TPU v7x, 256 devices: a whole 4x4x8 slice. The times are simulated.
256 devices in a mesh: half: 2 (over z_lo), row: 8 (over z_hi, core), col: 16 (over y, x).
Axes of the slice: x: 4, y: 4, z: 8 (z_hi: 4, z_lo: 2; z = z_hi * 2 + z_lo), core: 2. Of those that a mesh axis runs over, the one named last changes fastest.
Arguments:
- root_factor: bfloat16 [3, 16, 128, 3, 16, 128], P(None, ('half', 'row'), None, None, 'col')
- root_pivots: float32 [3, 16, 128], P(None, ('half', 'row')), may hold values from -2 to 2
- child_factor: bfloat16 [2, 4, 8, 128, 2, 16, 128], P('half', None, 'row', None, None, 'col')
- child_pivots: float32 [2, 4, 8, 128], P('half', None, 'row'), may hold values from -2 to 2
- child_block: bfloat16 [2, 6, 8, 64, 2, 16, 128], P('half', None, 'row', None, None, 'col'), may hold values from -0.109375 to 0.109375
- child_rows: int32 [2, 3072], P('half'), may hold values from 0 to 6143, as said below
Outputs:
- root_inverse: float32 [6, 8, 128, 3, 16, 128], P(None, 'row', None, None, 'col')
- child_offdiag: float32 [2, 6, 8, 64, 2, 16, 128], P('half', None, 'row', None, None, 'col')
- child_inverse: float32 [2, 4, 8, 128, 2, 16, 128], P('half', None, 'row', None, None, 'col')
Inputs may be any that keep to these rules, and one draw needn't show every extreme that they name: root_factor read as a 6144 x 6144 matrix and each child_factor[c] read as a 4096 x 4096 matrix are unit lower triangular (ones on the diagonal, zeros above it). Entry i of child_rows[c] lies in root rows 128 * k to 128 * k + 127 for k = i // 64; every such block contributes its first and its last row; entries of one child are distinct and ascending.
All inputs are finite; a program needn't handle non-finite values.
Results may differ from a plain program's by a relative error of at most 0.0041.
Values may be sent and summed in bfloat16 or wider, within the bound.
No kernel may reach another device: no remote copies, remote signals or barrier semaphores. Data moves between devices by JAX's collectives and lax.ppermute only.
A program may use at most 128 MiB of HBM per device.

v0:
```python
import functools

import jax
import jax.numpy as jnp
from jax import lax
from jax.experimental import pallas as pl
from jax.experimental.pallas import tpu as pltpu
from jax.sharding import PartitionSpec as P

AXES = ("half", "row", "col")
N_HALF, N_ROW, N_COL = 2, 8, 16
SIDE = 4
BLK = 128
REACH = 64
ROOT_PAIRS = [(0, 0), (1, 0), (1, 1), (2, 0), (2, 1), (2, 2)]
CHILD_PAIRS = [(0, 0), (1, 0), (2, 0), (2, 1), (3, 0), (3, 1)]
VMEM_LIMIT = 60 * 1024 * 1024


def permute(array, target):
    pairs = []
    for half in range(N_HALF):
        for row in range(N_ROW):
            for col in range(N_COL):
                to_half, to_row, to_col = target(half, row, col)
                pairs.append(
                    (
                        (half * N_ROW + row) * N_COL + col,
                        (to_half * N_ROW + to_row) * N_COL + to_col,
                    )
                )
    return lax.ppermute(array, AXES, pairs)


def along_x(step):
    return lambda h, r, q: (h, r, q // SIDE * SIDE + (q + step) % SIDE)


def along_y(step):
    return lambda h, r, q: (h, r, (q + SIDE * step) % N_COL)


def along_z(step):
    return lambda h, r, q: (h, (r + 2 * step) % N_ROW, q)


def other_core(h, r, q):
    return (h, r ^ 1, q)


def other_half(h, r, q):
    return (1 - h, r, q)


def mixed(r, p):
    return (r // 2 - p // 2) % SIDE * 2 + (r ^ p) % 2


def transposed_place(h, r, q):
    return (h, q % N_ROW, q // N_ROW * N_ROW + mixed(r, q % N_ROW))


def ring_parts(own, along, split):
    before = permute(own, along(1))
    after = permute(own, along(-1))
    if not split:
        return [own, after, permute(before, along(1)), before]
    cut = own.shape[0] // 2
    return [own, after, permute(before[:cut], along(1)), permute(after[cut:], along(-1)), before]


def plane_gather(first, second):
    one = jnp.stack(ring_parts(first, along_x, False))
    two = jnp.stack(ring_parts(second, along_y, False))
    return ring_parts(one, along_y, True), ring_parts(two, along_x, True)


def dot(left, right):
    return jnp.dot(left, right, preferred_element_type=jnp.float32)


def dot_nt(left, right):
    return lax.dot_general(left, right, (((1,), (1,)), ((), ())), preferred_element_type=jnp.float32)


def cat(parts, axis):
    return jnp.concatenate(parts, axis)


def load(pairs, sems):
    copies = [pltpu.make_async_copy(src, dst, sems.at[i]) for i, (src, dst) in enumerate(pairs)]
    for copy in copies:
        copy.start()
    for copy in copies:
        copy.wait()


def spread(parts, held):
    at = 0
    pairs = []
    for part in parts:
        pairs.append((part, held.at[pl.ds(at, part.shape[0])]))
        at += part.shape[0]
    return pairs


def chooser(ref, i):
    lanes = lax.broadcasted_iota(jnp.int32, (REACH, BLK), 1)
    return jnp.where(ref[pl.ds(i * REACH, REACH), :] == lanes, 1.0, 0.0).astype(jnp.bfloat16)


def pick(low_ref, ref, picked_ref):
    rows = cat(
        [dot(chooser(ref, i), low_ref[pl.ds(i * BLK, BLK), :]).astype(jnp.bfloat16) for i in range(6)], 0
    )
    for i in range(3):
        picked_ref[pl.ds(i * REACH, REACH), :] = dot_nt(
            chooser(ref, 6 + i), rows[:, i * BLK : (i + 1) * BLK]
        ).astype(jnp.bfloat16)


def prepare_kernel(shared, *refs):
    root_ref, root_scale, child_ref, child_scale, block_ref = refs[:5]
    turned_refs, right_refs = (refs[5:7], refs[7:]) if shared == 1 else (refs[5:6] * 2, refs[6:])
    if len(right_refs) == 1:
        right_refs = right_refs * 2
    turned_base = 0 if shared == 1 else 768
    right_base = 768 if shared == 1 else 0

    def tile(ref, i, j):
        return ref[pl.ds(i * BLK, BLK), pl.ds(j * BLK, BLK)]

    def factor(ref, scale_ref, pairs, turned, right, turned_at, right_at):
        for i, (a, b) in enumerate(pairs):
            scale = jnp.broadcast_to(scale_ref[pl.ds(a, 1), :], (BLK, BLK)).T
            own = tile(ref, a, b)
            turned[pl.ds(turned_at + i * BLK, BLK), :] = own.T
            right[pl.ds(right_at + i * BLK, BLK), :] = (scale * own.astype(jnp.float32)).astype(
                jnp.bfloat16
            )

    factor(root_ref, root_scale, ROOT_PAIRS, turned_refs[0], right_refs[0], 0, 0)
    factor(child_ref, child_scale, CHILD_PAIRS, turned_refs[1], right_refs[1], turned_base, right_base)
    sort = [block_ref[pl.ds(REACH * a, REACH), :] for a in (0, 2, 4, 1, 3, 5)]
    for j in range(3):
        pair = cat(sort[2 * j : 2 * j + 2], 0)
        for i in range(2):
            at = 768 + j * 2 * BLK + i * BLK
            turned_refs[1][pl.ds(turned_base + at, BLK), :] = tile(block_ref, j, i).T
            right_refs[1][pl.ds(right_base + at, BLK), :] = pair[:, i * BLK : (i + 1) * BLK].T


def root_kernel(slot_one, slot_two, *refs):
    parts, right_in, other_picks, my_picks = refs[:10], refs[10], refs[11], refs[12]
    out_ref, theirs_ref, mine_ref, one_ref, two_ref, right_ref, acc, sems = refs[13:]
    right_in = right_in.at[:, pl.ds(0, 768), :]
    load(spread(parts[:5], one_ref) + spread(parts[5:], two_ref) + [(right_in, right_ref)], sems)
    acc[...] = jnp.zeros_like(acc)

    def step(i):
        pair = (2 * i, 2 * i + 1)
        right = [[right_ref[r, pl.ds(BLK * k, BLK), :] for k in range(6)] for r in pair]
        right_0 = cat([right[0][0], right[1][0]], 0)
        right_1 = cat([cat(right[k][1:3], 1) for k in range(2)], 0)
        right_2 = cat([cat(right[k][3:6], 1) for k in range(2)], 0)
        for side in range(2):
            one = [slot_one[side * N_ROW + r] for r in pair]
            two = [slot_two[side * N_ROW + r] for r in pair]
            left_1 = cat([one_ref[one[k]] for k in range(2)], 1)
            left_2 = cat([two_ref[two[k]] for k in range(2)], 1)
            acc[side] += dot(left_2, right_2)
            acc[side, : 2 * BLK, : 2 * BLK] += dot(left_1[BLK:], right_1)
            acc[side, :BLK, :BLK] += dot(left_1[:BLK], right_0)

    for i in range(N_ROW // 2):
        step(i)
    for outer in range(3):
        for side in range(2):
            out_ref[pl.ds((2 * outer + side) * BLK, BLK), :] = acc[
                side, pl.ds(outer * BLK, BLK), :
            ].astype(out_ref.dtype)
    pick(out_ref, other_picks, theirs_ref)
    pick(out_ref, my_picks, mine_ref)


def sum_kernel(mine_ref, other_ref, out_ref):
    for i in range(3):
        lanes = pl.ds(i * BLK, BLK)
        out_ref[pl.ds(i, 768, stride=3), :] = mine_ref[:, lanes].astype(jnp.float32) + other_ref[
            :, lanes
        ].astype(jnp.float32)


def offdiag_kernel(slot_one, slot_two, *refs):
    parts, (right_in, out_ref, low_ref, one_ref, two_ref, block_ref, acc, sems) = refs[:10], refs[10:]
    block_in = right_in.at[:, pl.ds(1536, 768), :]
    load(spread(parts[:5], one_ref) + spread(parts[5:], two_ref) + [(block_in, block_ref)], sems)
    acc[...] = jnp.zeros_like(acc)

    def step(r):
        left = cat([block_ref[r, pl.ds(256 * i, 256), :] for i in range(3)], 1)
        right = cat(
            [
                one_ref[slot_one[r]],
                two_ref[slot_two[r]],
                one_ref[slot_one[N_ROW + r]],
                two_ref[slot_two[N_ROW + r]],
            ],
            0,
        )
        acc[...] += dot(left, right)

    for i in range(N_ROW):
        step(i)
    total = -acc[...]
    low_ref[...] = total.astype(low_ref.dtype)
    for i in range(2):
        out_ref[pl.ds(i, 384, stride=2), :] = total[i * BLK : (i + 1) * BLK, :].T


def child_kernel(slots, part_slots, *refs):
    parts, (left_in, right_in, out_ref, left_ref, factor_ref, right_ref, acc, sems) = refs[:10], refs[10:]
    first, second = pl.ds(0, 768), pl.ds(768, 768)
    pairs = [
        (left_in.at[:, first, :], left_ref.at[:, first, :]),
        (right_in.at[:, pl.ds(768, 768), :], factor_ref),
        (left_in.at[:, second, :], left_ref.at[:, second, :]),
    ]
    at = 0
    for part in parts:
        pairs.append((part, right_ref.at[at // 256, pl.ds(at % 256, part.shape[0]), :]))
        at += part.shape[0]
    copies = [pltpu.make_async_copy(src, dst, sems.at[i]) for i, (src, dst) in enumerate(pairs)]
    for copy in copies:
        copy.start()
    acc[...] = jnp.zeros_like(acc)
    for copy in copies[:2]:
        copy.wait()

    def own(r):
        right = [factor_ref[r, pl.ds(BLK * i, BLK), :] for i in range(6)]
        right_0 = cat(right[0:2], 0)
        right_1 = cat([cat(right[2:4], 1), cat(right[4:6], 1)], 0)
        for side in range(2):
            slot = slots[side * N_ROW + r]
            left_0 = cat([left_ref[slot, :BLK, :], left_ref[slot, BLK : 2 * BLK, :]], 1)
            left_1 = cat([left_ref[slot, 2 * BLK : 4 * BLK, :], left_ref[slot, 4 * BLK : 6 * BLK, :]], 1)
            acc[side] += dot(left_1, right_1)
            acc[side, :BLK, :BLK] += dot(left_0, right_0)

    for r in range(N_ROW):
        own(r)
    for copy in copies[2:]:
        copy.wait()

    def coupled(i):
        pair = (2 * i, 2 * i + 1)
        right = cat([right_ref[part_slots[r]] for r in pair], 1)
        for side in range(2):
            held = [slots[side * N_ROW + r] for r in pair]
            left = cat([left_ref[slot, pl.ds(768 + 256 * k, 256), :] for slot in held for k in range(3)], 1)
            acc[side] -= dot_nt(left, right)

    for i in range(N_ROW // 2):
        coupled(i)
    for outer in range(2):
        for side in range(2):
            for i in range(2):
                at = (2 * outer + side) * 2 * BLK + i
                out_ref[pl.ds(at, BLK, stride=2), :] = acc[
                    side, pl.ds(outer * BLK, BLK), pl.ds(i * BLK, BLK)
                ]


def call(kernel, scalars, arrays, outs, scratch, blocks=()):
    vmem = pl.BlockSpec(memory_space=pltpu.VMEM)
    smem = pl.BlockSpec(memory_space=pltpu.SMEM)
    anywhere = pl.BlockSpec(memory_space=pl.ANY)
    return pl.pallas_call(
        kernel,
        in_specs=[smem] * len(scalars) + [anywhere] * len(arrays) + [vmem] * len(blocks),
        out_specs=[vmem] * len(outs),
        out_shape=[jax.ShapeDtypeStruct(*o) for o in outs],
        scratch_shapes=list(scratch),
        compiler_params=pltpu.CompilerParams(vmem_limit_bytes=VMEM_LIMIT),
    )(*scalars, *arrays, *blocks)


def per_device(root_factor, root_pivots, child_factor, child_pivots, child_block, child_rows):
    row = lax.axis_index("row")
    col = lax.axis_index("col")
    bf16 = jnp.bfloat16
    root_turned, child_turned, right_here = call(
        functools.partial(prepare_kernel, 1),
        (),
        (),
        [((768, BLK), bf16), ((1536, BLK), bf16), ((2304, BLK), bf16)],
        (),
        (
            root_factor.reshape(384, 384),
            root_pivots.reshape(3, BLK),
            child_factor.reshape(512, 256),
            child_pivots.reshape(4, BLK),
            child_block.reshape(384, 256),
        ),
    )
    turned = permute(root_turned, transposed_place)
    right = lax.all_gather(right_here, "row", axis=0, tiled=False)

    rows = child_rows[0].reshape(48, REACH) % BLK
    row_picks = lax.dynamic_index_in_dim(rows.reshape(6, N_ROW, REACH), row, 1, keepdims=False)
    col_picks = lax.dynamic_index_in_dim(rows.reshape(3, N_COL, REACH), col, 1, keepdims=False)
    my_picks = jnp.concatenate([row_picks.reshape(-1), col_picks.reshape(-1)])[:, None]
    other_picks = permute(my_picks, other_half)
    child_turned = lax.optimization_barrier((child_turned, other_picks))[0]
    child_here = permute(child_turned, transposed_place)

    side = jnp.arange(2, dtype=jnp.int32)[:, None]
    classes = jnp.arange(N_ROW, dtype=jnp.int32)[None, :]
    source = side * N_ROW + mixed(classes, row)
    my_x, my_y = col % SIDE, col // SIDE

    def plane_slots(place):
        dx = (place % SIDE - my_x) % SIDE
        dy = (place // SIDE - my_y) % SIDE
        return (dy * SIDE + dx).reshape(-1), (dx * SIDE + dy).reshape(-1)

    root_slots = plane_slots(source)
    offdiag_slots = plane_slots(side * N_ROW + classes)
    slots = source.reshape(-1)
    r = classes[0]
    part_slots = ((r ^ row) & 1) * SIDE + (r // 2 - row // 2) % SIDE
    turned, root_slots, offdiag_slots, slots, part_slots, my_picks, other_picks = lax.optimization_barrier(
        (turned, root_slots, offdiag_slots, slots, part_slots, my_picks, other_picks)
    )
    root_parts = plane_gather(turned[:384], turned[384:])
    child_here = lax.optimization_barrier((child_here, root_parts))[0]
    child_left = lax.all_gather(child_here, "col", axis=0, tiled=False)

    partial, theirs, mine = call(
        root_kernel,
        root_slots,
        (*root_parts[0], *root_parts[1], right),
        [((768, 384), bf16), ((192, 384), bf16), ((192, 384), bf16)],
        [
            pltpu.VMEM((N_COL, 384, BLK), bf16),
            pltpu.VMEM((N_COL, 384, BLK), bf16),
            pltpu.VMEM((N_ROW, 768, BLK), bf16),
            pltpu.VMEM((2, 384, 384), jnp.float32),
            pltpu.SemaphoreType.DMA((11,)),
        ],
        (other_picks, my_picks),
    )
    theirs = permute(theirs, other_half)
    picked = (mine.astype(jnp.float32) + theirs.astype(jnp.float32)).astype(bf16)
    late = lax.optimization_barrier((partial, picked))[0]
    late = permute(late, other_half)
    (root_inverse,) = call(sum_kernel, (), (), [((2304, BLK), jnp.float32)], (), (partial, late))
    picked_parts = plane_gather(picked[:96], picked[96:])
    offdiag, offdiag_low = call(
        offdiag_kernel,
        offdiag_slots,
        (*picked_parts[0], *picked_parts[1], right),
        [((768, BLK), jnp.float32), ((256, 384), bf16)],
        [
            pltpu.VMEM((N_COL, 96, 384), bf16),
            pltpu.VMEM((N_COL, 96, 384), bf16),
            pltpu.VMEM((N_ROW, 768, BLK), bf16),
            pltpu.VMEM((256, 384), jnp.float32),
            pltpu.SemaphoreType.DMA((11,)),
        ],
    )
    offdiag_low = lax.optimization_barrier((offdiag_low, late))[0]
    line = ring_parts(offdiag_low, along_z, True)
    ready = lax.optimization_barrier((line, root_inverse))[0]
    parts = line + [permute(part, other_core) for part in ready]
    (child_inverse,) = call(
        child_kernel,
        (slots, part_slots),
        (*parts, child_left, right),
        [((1024, BLK), jnp.float32)],
        [
            pltpu.VMEM((N_COL, 1536, BLK), bf16),
            pltpu.VMEM((N_ROW, 768, BLK), bf16),
            pltpu.VMEM((N_ROW, 256, 384), bf16),
            pltpu.VMEM((2, 256, 256), jnp.float32),
            pltpu.SemaphoreType.DMA((13,)),
        ],
    )
    return (
        root_inverse.reshape(6, 1, BLK, 3, 1, BLK),
        offdiag.reshape(child_block.shape),
        child_inverse.reshape(child_factor.shape),
    )


def solution(mesh):
    return jax.shard_map(
        per_device,
        mesh=mesh,
        in_specs=(
            P(None, ("half", "row"), None, None, "col", None),
            P(None, ("half", "row"), None),
            P("half", None, "row", None, None, "col", None),
            P("half", None, "row", None),
            P("half", None, "row", None, None, "col", None),
            P("half", None),
        ),
        out_specs=(
            P(None, "row", None, None, "col", None),
            P("half", None, "row", None, None, "col", None),
            P("half", None, "row", None, None, "col", None),
        ),
        check_vma=False,
    )
```

profile of v0, /device:TPU:1, one launch (start us, length us, event | category | flops | bytes accessed | tf_op | source)
XLA Modules:
  0.0 202.2 jit_solution(1283508098417864982)
XLA Ops:
  7.2 1.3 copy.30
  8.5 1.6 copy.29
  10.1 1.7 copy.28
  11.8 1.2 copy.13
  13.8 2.6 %shard_map.85 = (bf16[768,128]{1,0:T(8,128)(2,1)}, bf16[1536,128]{1,0:T(8,128)(2,1)}, bf16[2304,128]{1,0:T(8,128)(2,1)}) custom-call(bf16[384,384]{1,0:T(8,128)(2,1)} %bitcast.58, f32[3,128]{1,0:T(4,128)} %bitcast.77, bf16[512,256]{1,0:T(8,128)(2,1)} %bitcast.59, f32[4,128]{1,0:T(4,128)} %bitcast.78, bf16[384,256]{1,0:T(8,128)(2,1)} %bitcast.60), custom_call_target="tpu_custom_call" | custom-call | tf_op jit(solution)/shard_map/pallas_call | solution.py:279
  16.9 1.4 reduce.9
  19.6 2.6 %collective-permute-start.1 = (s32[576,1]{1,0:T(8,128)S(1)}, s32[576,1]{1,0:T(8,128)S(1)}, u32[]{:S(2)}, u32[]{:S(2)}) collective-permute-start(s32[576,1]{1,0:T(8,128)S(1)} %copy.14), channel_id=1, source_target_pairs={{0,128},{1,129},{2,130},{3,131},{4,132},{5,133},{6,134},{7,135},{8... | collective-permute-start | bytes 6920 | tf_op jit(solution)/shard_map/ppermute | solution.py:32
  22.2 3.9 %collective-permute-start = (bf16[768,128]{1,0:T(8,128)(2,1)}, bf16[768,128]{1,0:T(8,128)(2,1)S(1)}, u32[]{:S(2)}, u32[]{:S(2)}) collective-permute-start(bf16[768,128]{1,0:T(8,128)(2,1)} %get-tuple-element.29), channel_id=1, source_target_pairs={{0,0},{1,17},{2,38},{3,55},{4,68},{5,85},{6,98},{7,115},{8,8},{9,2... | collective-permute-start | bytes 589832 | tf_op jit(solution)/shard_map/ppermute | solution.py:32
  30.1 12.9 %collective-permute-start.10 = (bf16[384,128]{1,0:T(8,128)(2,1)S(1)}, bf16[384,128]{1,0:T(8,128)(2,1)S(1)}, u32[]{:S(2)}, u32[]{:S(2)}) collective-permute-start(bf16[384,128]{1,0:T(8,128)(2,1)S(1)} %get-tuple-element.69), channel_id=1, source_target_pairs={{0,4},{1,5},{2,6},{3,7},{4,8},{5,9},{6,10},{7,11},{8,12},{9,13},{1... | collective-permute-start | bytes 294920 | tf_op jit(solution)/shard_map/ppermute | solution.py:32
  43.0 15.4 %collective-permute-start.2 = (bf16[384,128]{1,0:T(8,128)(2,1)S(1)}, bf16[384,128]{1,0:T(8,128)(2,1)S(1)}, u32[]{:S(2)}, u32[]{:S(2)}) collective-permute-start(bf16[384,128]{1,0:T(8,128)(2,1)S(1)} %get-tuple-element.70), channel_id=1, source_target_pairs={{0,3},{1,0},{2,1},{3,2},{4,7},{5,4},{6,5},{7,6},{8,11},{9,8},{10,9... | collective-permute-start | bytes 294920 | tf_op jit(solution)/shard_map/ppermute | solution.py:32
  58.4 3.9 %collective-permute-start.9 = (bf16[384,128]{1,0:T(8,128)(2,1)S(1)}, bf16[384,128]{1,0:T(8,128)(2,1)S(1)}, u32[]{:S(2)}, u32[]{:S(2)}) collective-permute-start(bf16[384,128]{1,0:T(8,128)(2,1)S(1)} %get-tuple-element.69), channel_id=1, source_target_pairs={{0,12},{1,13},{2,14},{3,15},{4,0},{5,1},{6,2},{7,3},{8,4},{9,5},{1... | collective-permute-start | bytes 294920 | tf_op jit(solution)/shard_map/ppermute | solution.py:32
  62.4 1.1 collective-permute-done.4
  63.5 2.3 %collective-permute-start.6 = (bf16[4,384,128]{2,1,0:T(8,128)(2,1)S(1)}, bf16[4,384,128]{2,1,0:T(8,128)(2,1)S(1)}, u32[]{:S(2)}, u32[]{:S(2)}) collective-permute-start(bf16[4,384,128]{2,1,0:T(8,128)(2,1)S(1)} %pad_maximum_fusion.refs_0_), channel_id=1, source_target_pairs={{0,4},{1,5},{2,6},{3,7},{4,8},{5,9},{6,10},{7,11},{8,12},{9,13},{1... | collective-permute-start | bytes 1179656 | tf_op jit(solution)/shard_map/ppermute | solution.py:32
  65.9 1.8 collective-permute-start.5
  67.9 2.7 %collective-permute-start.12 = (bf16[4,384,128]{2,1,0:T(8,128)(2,1)S(1)}, bf16[4,384,128]{2,1,0:T(8,128)(2,1)S(1)}, u32[]{:S(2)}, u32[]{:S(2)}) collective-permute-start(bf16[4,384,128]{2,1,0:T(8,128)(2,1)S(1)} %pad_maximum_fusion.1.refs_5_), channel_id=1, source_target_pairs={{0,3},{1,0},{2,1},{3,2},{4,7},{5,4},{6,5},{7,6},{8,11},{9,8},{10,9... | collective-permute-start | bytes 1179656 | tf_op jit(solution)/shard_map/ppermute | solution.py:32
  70.6 5.0 %collective-permute-start.41 = (bf16[1536,128]{1,0:T(8,128)(2,1)}, bf16[1536,128]{1,0:T(8,128)(2,1)S(1)}, u32[]{:S(2)}, u32[]{:S(2)}) collective-permute-start(bf16[1536,128]{1,0:T(8,128)(2,1)} %get-tuple-element.53), channel_id=1, source_target_pairs={{0,0},{1,17},{2,38},{3,55},{4,68},{5,85},{6,98},{7,115},{8,8},{9,2... | collective-permute-start | bytes 1179656 | tf_op jit(solution)/shard_map/ppermute | solution.py:32
  75.5 1.4 collective-permute-done.6.refs_4_
  76.9 1.3 collective-permute-start.7
  78.2 2.0 collective-permute-start.8
  81.7 2.7 %collective-permute-start.15 = (bf16[2,384,128]{2,1,0:T(8,128)(2,1)}, bf16[2,384,128]{2,1,0:T(8,128)(2,1)}, u32[]{:S(2)}, u32[]{:S(2)}) collective-permute-start(bf16[2,384,128]{2,1,0:T(8,128)(2,1)} %slice.59), channel_id=1, source_target_pairs={{0,3},{1,0},{2,1},{3,2},{4,7},{5,4},{6,5},{7,6},{8,11},{9,8},{10,9... | collective-permute-start | bytes 589832 | tf_op jit(solution)/shard_map/ppermute | solution.py:32
  84.4 5.3 %collective-permute-done.41 = bf16[1536,128]{1,0:T(8,128)(2,1)S(1)} collective-permute-done((bf16[1536,128]{1,0:T(8,128)(2,1)}, bf16[1536,128]{1,0:T(8,128)(2,1)S(1)}, u32[]{:S(2)}, u32[]{:S(2)}) %collective-permute-start.41) | collective-permute-done | bytes 393248 | tf_op jit(solution)/shard_map/ppermute | solution.py:32
  89.7 1.4 collective-permute-done.7.refs_2_
  91.1 1.4 collective-permute-done.15.refs_8_
  93.4 9.3 %all-gather.5.cloned.1.call-done = bf16[18432,128]{1,0:T(8,128)(2,1)} async-done(((bf16[2304,128]{1,0:T(8,128)(2,1)}), bf16[18432,128]{1,0:T(8,128)(2,1)}) %all-gather.5.cloned.1.call-update) | async-done | bytes 4718608 | tf_op jit(solution)/shard_map/all_gather | solution.py:308
  102.8 6.3 %shard_map.86 = (bf16[768,384]{1,0:T(8,128)(2,1)}, bf16[192,384]{1,0:T(8,128)(2,1)}, bf16[192,384]{1,0:T(8,128)(2,1)}) custom-call(s32[16]{0:T(128)} %multiply_add_fusion.4.slot_one, s32[16]{0:T(128)} %get-tuple-element.31.slot_two, bf16[4,384,128]{2,1,0:T(8,128)(2,1)} %copy-done, bf16[4,384,128]{2,1,0:T(8,128)(2,1)} %copy-done.5, ...), custom_call_target="tpu_custom_call" | custom-call | tf_op jit(solution)/shard_map/pallas_call | solution.py:279
  109.1 7.0 %collective-permute-start.16 = (bf16[192,384]{1,0:T(8,128)(2,1)}, bf16[192,384]{1,0:T(8,128)(2,1)S(1)}, u32[]{:S(2)}, u32[]{:S(2)}) collective-permute-start(bf16[192,384]{1,0:T(8,128)(2,1)} %get-tuple-element.38), channel_id=1, source_target_pairs={{0,128},{1,129},{2,130},{3,131},{4,132},{5,133},{6,134},{7,135},{8... | collective-permute-start | bytes 442376 | tf_op jit(solution)/shard_map/ppermute | solution.py:32
  116.2 3.6 %collective-permute-done.16 = bf16[192,384]{1,0:T(8,128)(2,1)S(1)} collective-permute-done((bf16[192,384]{1,0:T(8,128)(2,1)}, bf16[192,384]{1,0:T(8,128)(2,1)S(1)}, u32[]{:S(2)}, u32[]{:S(2)}) %collective-permute-start.16) | collective-permute-done | bytes 147488 | tf_op jit(solution)/shard_map/ppermute | solution.py:32
  120.9 4.0 %collective-permute-start.18 = (bf16[96,384]{1,0:T(8,128)(2,1)S(1)}, bf16[96,384]{1,0:T(8,128)(2,1)S(1)}, u32[]{:S(2)}, u32[]{:S(2)}) collective-permute-start(bf16[96,384]{1,0:T(8,128)(2,1)S(1)} %get-tuple-element.74), channel_id=1, source_target_pairs={{0,3},{1,0},{2,1},{3,2},{4,7},{5,4},{6,5},{7,6},{8,11},{9,8},{10,9... | collective-permute-start | bytes 221192 | tf_op jit(solution)/shard_map/ppermute | solution.py:32
  124.9 1.3 collective-permute-done.19
  126.3 4.1 %collective-permute-start.25 = (bf16[96,384]{1,0:T(8,128)(2,1)S(1)}, bf16[96,384]{1,0:T(8,128)(2,1)S(1)}, u32[]{:S(2)}, u32[]{:S(2)}) collective-permute-start(bf16[96,384]{1,0:T(8,128)(2,1)S(1)} %get-tuple-element.73), channel_id=1, source_target_pairs={{0,12},{1,13},{2,14},{3,15},{4,0},{5,1},{6,2},{7,3},{8,4},{9,5},{1... | collective-permute-start | bytes 221192 | tf_op jit(solution)/shard_map/ppermute | solution.py:32
  131.5 3.4 %collective-permute-start.21 = (bf16[4,96,384]{2,1,0:T(8,128)(2,1)S(1)}, bf16[4,96,384]{2,1,0:T(8,128)(2,1)S(1)}, u32[]{:S(2)}, u32[]{:S(2)}) collective-permute-start(bf16[4,96,384]{2,1,0:T(8,128)(2,1)S(1)} %pad_maximum_fusion.2.refs_0_), channel_id=1, source_target_pairs={{0,12},{1,13},{2,14},{3,15},{4,0},{5,1},{6,2},{7,3},{8,4},{9,5},{1... | collective-permute-start | bytes 884744 | tf_op jit(solution)/shard_map/ppermute | solution.py:32
  135.0 1.1 collective-permute-done.27
  136.1 2.1 %collective-permute-start.29 = (bf16[4,96,384]{2,1,0:T(8,128)(2,1)S(1)}, bf16[4,96,384]{2,1,0:T(8,128)(2,1)S(1)}, u32[]{:S(2)}, u32[]{:S(2)}) collective-permute-start(bf16[4,96,384]{2,1,0:T(8,128)(2,1)S(1)} %pad_maximum_fusion.3.refs_5_), channel_id=1, source_target_pairs={{0,1},{1,2},{2,3},{3,0},{4,5},{5,6},{6,7},{7,4},{8,9},{9,10},{10,1... | collective-permute-start | bytes 884744 | tf_op jit(solution)/shard_map/ppermute | solution.py:32
  138.9 3.0 %collective-permute-done.22.refs_4_ = bf16[4,96,384]{2,1,0:T(8,128)(2,1)S(1)} collective-permute-done((bf16[4,96,384]{2,1,0:T(8,128)(2,1)S(1)}, bf16[4,96,384]{2,1,0:T(8,128)(2,1)S(1)}, u32[]{:S(2)}, u32[]{:S(2)}) %collective-permute-start.22) | collective-permute-done | bytes 294944 | tf_op jit(solution)/shard_map/ppermute | solution.py:32
  142.3 2.7 %collective-permute-start.24 = (bf16[2,96,384]{2,1,0:T(8,128)(2,1)S(1)}, bf16[2,96,384]{2,1,0:T(8,128)(2,1)S(1)}, u32[]{:S(2)}, u32[]{:S(2)}) collective-permute-start(bf16[2,96,384]{2,1,0:T(8,128)(2,1)S(1)} %slice.62), channel_id=1, source_target_pairs={{0,12},{1,13},{2,14},{3,15},{4,0},{5,1},{6,2},{7,3},{8,4},{9,5},{1... | collective-permute-start | bytes 442376 | tf_op jit(solution)/shard_map/ppermute | solution.py:32
  145.0 2.6 %collective-permute-start.30 = (bf16[2,96,384]{2,1,0:T(8,128)(2,1)S(1)}, bf16[2,96,384]{2,1,0:T(8,128)(2,1)S(1)}, u32[]{:S(2)}, u32[]{:S(2)}) collective-permute-start(bf16[2,96,384]{2,1,0:T(8,128)(2,1)S(1)} %slice.64), channel_id=1, source_target_pairs={{0,1},{1,2},{2,3},{3,0},{4,5},{5,6},{6,7},{7,4},{8,9},{9,10},{10,1... | collective-permute-start | bytes 442376 | tf_op jit(solution)/shard_map/ppermute | solution.py:32
  147.9 2.7 %collective-permute-done.30.refs_7_ = bf16[2,96,384]{2,1,0:T(8,128)(2,1)S(1)} collective-permute-done((bf16[2,96,384]{2,1,0:T(8,128)(2,1)S(1)}, bf16[2,96,384]{2,1,0:T(8,128)(2,1)S(1)}, u32[]{:S(2)}, u32[]{:S(2)}) %collective-permute-start.30) | collective-permute-done | bytes 147488 | tf_op jit(solution)/shard_map/ppermute | solution.py:32
  150.6 2.3 %collective-permute-done.31.refs_8_ = bf16[2,96,384]{2,1,0:T(8,128)(2,1)S(1)} collective-permute-done((bf16[2,96,384]{2,1,0:T(8,128)(2,1)S(1)}, bf16[2,96,384]{2,1,0:T(8,128)(2,1)S(1)}, u32[]{:S(2)}, u32[]{:S(2)}) %collective-permute-start.31) | collective-permute-done | bytes 147488 | tf_op jit(solution)/shard_map/ppermute | solution.py:32
  153.6 4.9 %shard_map.88 = (f32[768,128]{1,0:T(8,128)}, bf16[256,384]{1,0:T(8,128)(2,1)}) custom-call(s32[16]{0:T(128)} %multiply_add_fusion.2.slot_one, s32[16]{0:T(128)} %get-tuple-element.41.slot_two, bf16[4,96,384]{2,1,0:T(8,128)(2,1)} %copy-done.2, bf16[4,96,384]{2,1,0:T(8,128)(2,1)} %copy-done.9, bf16[2,96,384]{2,1,0:T(8,128)(2,1)} %copy-done.20, ...), custom_call_target="tpu_custom_call" | custom-call | tf_op jit(solution)/shard_map/pallas_call | solution.py:279
  158.6 3.2 %collective-permute-start.33 = (bf16[256,384]{1,0:T(8,128)(2,1)}, bf16[256,384]{1,0:T(8,128)(2,1)S(1)}, u32[]{:S(2)}, u32[]{:S(2)}) collective-permute-start(bf16[256,384]{1,0:T(8,128)(2,1)} %get-tuple-element.47.refs_0_), channel_id=1, source_target_pairs={{0,32},{1,33},{2,34},{3,35},{4,36},{5,37},{6,38},{7,39},{8,40},{9,... | collective-permute-start | bytes 589832 | tf_op jit(solution)/shard_map/ppermute | solution.py:32
  162.2 3.5 %collective-permute-done.33.refs_4_ = bf16[256,384]{1,0:T(8,128)(2,1)S(1)} collective-permute-done((bf16[256,384]{1,0:T(8,128)(2,1)}, bf16[256,384]{1,0:T(8,128)(2,1)S(1)}, u32[]{:S(2)}, u32[]{:S(2)}) %collective-permute-start.33) | collective-permute-done | bytes 196640 | tf_op jit(solution)/shard_map/ppermute | solution.py:32
  165.7 2.3 %collective-permute-start.34 = (bf16[128,384]{1,0:T(8,128)(2,1)S(1)}, bf16[128,384]{1,0:T(8,128)(2,1)S(1)}, u32[]{:S(2)}, u32[]{:S(2)}) collective-permute-start(bf16[128,384]{1,0:T(8,128)(2,1)S(1)} %slice.66), channel_id=1, source_target_pairs={{0,32},{1,33},{2,34},{3,35},{4,36},{5,37},{6,38},{7,39},{8,40},{9,... | collective-permute-start | bytes 294920 | tf_op jit(solution)/shard_map/ppermute | solution.py:32
  168.0 1.4 collective-permute-start.35
  169.5 2.4 %shard_map.87 = f32[2304,128]{1,0:T(8,128)} custom-call(bf16[768,384]{1,0:T(8,128)(2,1)} %get-tuple-element.39.mine_ref, bf16[768,384]{1,0:T(8,128)(2,1)} %copy-done.12), custom_call_target="tpu_custom_call" | custom-call | tf_op jit(solution)/shard_map/pallas_call | solution.py:279
  171.9 2.0 collective-permute-done.34.refs_2_
  173.8 3.9 %collective-permute-done.35.refs_3_ = bf16[128,384]{1,0:T(8,128)(2,1)S(1)} collective-permute-done((bf16[128,384]{1,0:T(8,128)(2,1)S(1)}, bf16[128,384]{1,0:T(8,128)(2,1)S(1)}, u32[]{:S(2)}, u32[]{:S(2)}) %collective-permute-start.35) | collective-permute-done | bytes 98336 | tf_op jit(solution)/shard_map/ppermute | solution.py:32
  177.7 8.5 %collective-permute-start.36 = (bf16[256,384]{1,0:T(8,128)(2,1)}, bf16[256,384]{1,0:T(8,128)(2,1)S(1)}, u32[]{:S(2)}, u32[]{:S(2)}) collective-permute-start(bf16[256,384]{1,0:T(8,128)(2,1)} %get-tuple-element.47.refs_0_), channel_id=1, source_target_pairs={{0,16},{1,17},{2,18},{3,19},{4,20},{5,21},{6,22},{7,23},{8,24},{9,... | collective-permute-start | bytes 589832 | tf_op jit(solution)/shard_map/ppermute | solution.py:32
  189.1 6.2 %shard_map.89 = f32[1024,128]{1,0:T(8,128)} custom-call(s32[16]{0:T(128)} %copy-done.28, s32[8]{0:T(128)} %multiply_add_fusion.part_slots, bf16[256,384]{1,0:T(8,128)(2,1)} %get-tuple-element.47.refs_0_, bf16[256,384]{1,0:T(8,128)(2,1)} %copy-done.14, bf16[128,384]{1,0:T(8,128)(2,1)} %copy-done.24, bf16[128,384]{1,0:T(8,128)(2,1)} %copy-done.25, ...), custom_call_target="tpu_custom_call" | custom-call | tf_op jit(solution)/shard_map/pallas_call | solution.py:279
  (152 shorter events, 16.9 us)
Async XLA Ops:
  7.2 95.6 %all-gather.5.cloned.1.call-start = ((), (), s32[]{:S(2)}) async-start(), calls=%async_computation | async-start | bytes 5308416 | tf_op jit(solution)/shard_map/all_gather | solution.py:308
  16.3 172.0 %all-gather.7.cloned.1.call-start = ((), (), s32[]{:S(2)}) async-start(), calls=%async_computation.1 | async-start | bytes 6684672 | tf_op jit(solution)/shard_map/all_gather | solution.py:338
  19.6 9.0 %collective-permute-start.1 = (s32[576,1]{1,0:T(8,128)S(1)}, s32[576,1]{1,0:T(8,128)S(1)}, u32[]{:S(2)}, u32[]{:S(2)}) collective-permute-start(s32[576,1]{1,0:T(8,128)S(1)} %copy.14), channel_id=1, source_target_pairs={{0,128},{1,129},{2,130},{3,131},{4,132},{5,133},{6,134},{7,135},{8... | collective-permute-start | bytes 6920 | tf_op jit(solution)/shard_map/ppermute | solution.py:32
  22.2 6.9 %collective-permute-start = (bf16[768,128]{1,0:T(8,128)(2,1)}, bf16[768,128]{1,0:T(8,128)(2,1)S(1)}, u32[]{:S(2)}, u32[]{:S(2)}) collective-permute-start(bf16[768,128]{1,0:T(8,128)(2,1)} %get-tuple-element.29), channel_id=1, source_target_pairs={{0,0},{1,17},{2,38},{3,55},{4,68},{5,85},{6,98},{7,115},{8,8},{9,2... | collective-permute-start | bytes 589832 | tf_op jit(solution)/shard_map/ppermute | solution.py:32
  26.4 82.7 %copy-start.28 = (s32[16]{0:T(128)}, s32[16]{0:T(128)S(1)}, u32[]{:S(2)}) copy-start(s32[16]{0:T(128)S(1)} %add.180.slots) | copy-start | bytes 196
  28.6 74.1 %copy-start.16 = (s32[576,1]{1,0:T(8,128)}, s32[576,1]{1,0:T(8,128)S(1)}, u32[]{:S(2)}) copy-start(s32[576,1]{1,0:T(8,128)S(1)} %collective-permute-done.1.refs_11_) | copy-start | bytes 6916
  29.1 29.3 %collective-permute-start.3 = (bf16[384,128]{1,0:T(8,128)(2,1)S(1)}, bf16[384,128]{1,0:T(8,128)(2,1)S(1)}, u32[]{:S(2)}, u32[]{:S(2)}) collective-permute-start(bf16[384,128]{1,0:T(8,128)(2,1)S(1)} %get-tuple-element.70), channel_id=1, source_target_pairs={{0,1},{1,2},{2,3},{3,0},{4,5},{5,6},{6,7},{7,4},{8,9},{9,10},{10,1... | collective-permute-start | bytes 294920 | tf_op jit(solution)/shard_map/ppermute | solution.py:32
  30.1 32.2 %collective-permute-start.10 = (bf16[384,128]{1,0:T(8,128)(2,1)S(1)}, bf16[384,128]{1,0:T(8,128)(2,1)S(1)}, u32[]{:S(2)}, u32[]{:S(2)}) collective-permute-start(bf16[384,128]{1,0:T(8,128)(2,1)S(1)} %get-tuple-element.69), channel_id=1, source_target_pairs={{0,4},{1,5},{2,6},{3,7},{4,8},{5,9},{6,10},{7,11},{8,12},{9,13},{1... | collective-permute-start | bytes 294920 | tf_op jit(solution)/shard_map/ppermute | solution.py:32
  43.0 19.3 %collective-permute-start.2 = (bf16[384,128]{1,0:T(8,128)(2,1)S(1)}, bf16[384,128]{1,0:T(8,128)(2,1)S(1)}, u32[]{:S(2)}, u32[]{:S(2)}) collective-permute-start(bf16[384,128]{1,0:T(8,128)(2,1)S(1)} %get-tuple-element.70), channel_id=1, source_target_pairs={{0,3},{1,0},{2,1},{3,2},{4,7},{5,4},{6,5},{7,6},{8,11},{9,8},{10,9... | collective-permute-start | bytes 294920 | tf_op jit(solution)/shard_map/ppermute | solution.py:32
  58.4 5.1 %collective-permute-start.4 = (bf16[384,128]{1,0:T(8,128)(2,1)S(1)}, bf16[384,128]{1,0:T(8,128)(2,1)S(1)}, u32[]{:S(2)}, u32[]{:S(2)}) collective-permute-start(bf16[384,128]{1,0:T(8,128)(2,1)S(1)} %collective-permute-done.3), channel_id=1, source_target_pairs={{0,1},{1,2},{2,3},{3,0},{4,5},{5,6},{6,7},{7,4},{8,9},{9,10},{10,1... | collective-permute-start | bytes 294920 | tf_op jit(solution)/shard_map/ppermute | solution.py:32
  58.4 9.3 %collective-permute-start.9 = (bf16[384,128]{1,0:T(8,128)(2,1)S(1)}, bf16[384,128]{1,0:T(8,128)(2,1)S(1)}, u32[]{:S(2)}, u32[]{:S(2)}) collective-permute-start(bf16[384,128]{1,0:T(8,128)(2,1)S(1)} %get-tuple-element.69), channel_id=1, source_target_pairs={{0,12},{1,13},{2,14},{3,15},{4,0},{5,1},{6,2},{7,3},{8,4},{9,5},{1... | collective-permute-start | bytes 294920 | tf_op jit(solution)/shard_map/ppermute | solution.py:32
  62.3 5.4 %collective-permute-start.11 = (bf16[384,128]{1,0:T(8,128)(2,1)S(1)}, bf16[384,128]{1,0:T(8,128)(2,1)S(1)}, u32[]{:S(2)}, u32[]{:S(2)}) collective-permute-start(bf16[384,128]{1,0:T(8,128)(2,1)S(1)} %collective-permute-done.10), channel_id=1, source_target_pairs={{0,4},{1,5},{2,6},{3,7},{4,8},{5,9},{6,10},{7,11},{8,12},{9,13},{1... | collective-permute-start | bytes 294920 | tf_op jit(solution)/shard_map/ppermute | solution.py:32
  63.5 39.2 %copy-start = (bf16[4,384,128]{2,1,0:T(8,128)(2,1)}, bf16[4,384,128]{2,1,0:T(8,128)(2,1)S(1)}, u32[]{:S(2)}) copy-start(bf16[4,384,128]{2,1,0:T(8,128)(2,1)S(1)} %pad_maximum_fusion.refs_0_) | copy-start | bytes 1179652
  63.5 13.4 %collective-permute-start.6 = (bf16[4,384,128]{2,1,0:T(8,128)(2,1)S(1)}, bf16[4,384,128]{2,1,0:T(8,128)(2,1)S(1)}, u32[]{:S(2)}, u32[]{:S(2)}) collective-permute-start(bf16[4,384,128]{2,1,0:T(8,128)(2,1)S(1)} %pad_maximum_fusion.refs_0_), channel_id=1, source_target_pairs={{0,4},{1,5},{2,6},{3,7},{4,8},{5,9},{6,10},{7,11},{8,12},{9,13},{1... | collective-permute-start | bytes 1179656 | tf_op jit(solution)/shard_map/ppermute | solution.py:32
  65.9 12.3 %collective-permute-start.5 = (bf16[4,384,128]{2,1,0:T(8,128)(2,1)S(1)}, bf16[4,384,128]{2,1,0:T(8,128)(2,1)S(1)}, u32[]{:S(2)}, u32[]{:S(2)}) collective-permute-start(bf16[4,384,128]{2,1,0:T(8,128)(2,1)S(1)} %pad_maximum_fusion.refs_0_), channel_id=1, source_target_pairs={{0,12},{1,13},{2,14},{3,15},{4,0},{5,1},{6,2},{7,3},{8,4},{9,5},{1... | collective-permute-start | bytes 1179656 | tf_op jit(solution)/shard_map/ppermute | solution.py:32
  67.8 34.9 %copy-start.1 = (bf16[4,384,128]{2,1,0:T(8,128)(2,1)}, bf16[4,384,128]{2,1,0:T(8,128)(2,1)S(1)}, u32[]{:S(2)}) copy-start(bf16[4,384,128]{2,1,0:T(8,128)(2,1)S(1)} %pad_maximum_fusion.1.refs_5_) | copy-start | bytes 1179652
  67.8 12.4 %collective-permute-start.13 = (bf16[4,384,128]{2,1,0:T(8,128)(2,1)S(1)}, bf16[4,384,128]{2,1,0:T(8,128)(2,1)S(1)}, u32[]{:S(2)}, u32[]{:S(2)}) collective-permute-start(bf16[4,384,128]{2,1,0:T(8,128)(2,1)S(1)} %pad_maximum_fusion.1.refs_5_), channel_id=1, source_target_pairs={{0,1},{1,2},{2,3},{3,0},{4,5},{5,6},{6,7},{7,4},{8,9},{9,10},{10,1... | collective-permute-start | bytes 1179656 | tf_op jit(solution)/shard_map/ppermute | solution.py:32
  67.9 13.0 %collective-permute-start.12 = (bf16[4,384,128]{2,1,0:T(8,128)(2,1)S(1)}, bf16[4,384,128]{2,1,0:T(8,128)(2,1)S(1)}, u32[]{:S(2)}, u32[]{:S(2)}) collective-permute-start(bf16[4,384,128]{2,1,0:T(8,128)(2,1)S(1)} %pad_maximum_fusion.1.refs_5_), channel_id=1, source_target_pairs={{0,3},{1,0},{2,1},{3,2},{4,7},{5,4},{6,5},{7,6},{8,11},{9,8},{10,9... | collective-permute-start | bytes 1179656 | tf_op jit(solution)/shard_map/ppermute | solution.py:32
  70.6 19.1 %collective-permute-start.41 = (bf16[1536,128]{1,0:T(8,128)(2,1)}, bf16[1536,128]{1,0:T(8,128)(2,1)S(1)}, u32[]{:S(2)}, u32[]{:S(2)}) collective-permute-start(bf16[1536,128]{1,0:T(8,128)(2,1)} %get-tuple-element.53), channel_id=1, source_target_pairs={{0,0},{1,17},{2,38},{3,55},{4,68},{5,85},{6,98},{7,115},{8,8},{9,2... | collective-permute-start | bytes 1179656 | tf_op jit(solution)/shard_map/ppermute | solution.py:32
  76.9 14.2 %collective-permute-start.7 = (bf16[2,384,128]{2,1,0:T(8,128)(2,1)S(1)}, bf16[2,384,128]{2,1,0:T(8,128)(2,1)}, u32[]{:S(2)}, u32[]{:S(2)}) collective-permute-start(bf16[2,384,128]{2,1,0:T(8,128)(2,1)S(1)} %slice.56), channel_id=1, source_target_pairs={{0,4},{1,5},{2,6},{3,7},{4,8},{5,9},{6,10},{7,11},{8,12},{9,13},{1... | collective-permute-start | bytes 589832 | tf_op jit(solution)/shard_map/ppermute | solution.py:32
  78.2 12.9 %collective-permute-start.8 = (bf16[2,384,128]{2,1,0:T(8,128)(2,1)S(1)}, bf16[2,384,128]{2,1,0:T(8,128)(2,1)}, u32[]{:S(2)}, u32[]{:S(2)}) collective-permute-start(bf16[2,384,128]{2,1,0:T(8,128)(2,1)S(1)} %slice.57), channel_id=1, source_target_pairs={{0,12},{1,13},{2,14},{3,15},{4,0},{5,1},{6,2},{7,3},{8,4},{9,5},{1... | collective-permute-start | bytes 589832 | tf_op jit(solution)/shard_map/ppermute | solution.py:32
  81.0 10.1 %collective-permute-start.14 = (bf16[2,384,128]{2,1,0:T(8,128)(2,1)}, bf16[2,384,128]{2,1,0:T(8,128)(2,1)}, u32[]{:S(2)}, u32[]{:S(2)}) collective-permute-start(bf16[2,384,128]{2,1,0:T(8,128)(2,1)} %slice.58), channel_id=1, source_target_pairs={{0,1},{1,2},{2,3},{3,0},{4,5},{5,6},{6,7},{7,4},{8,9},{9,10},{10,1... | collective-permute-start | bytes 589832 | tf_op jit(solution)/shard_map/ppermute | solution.py:32
  81.7 10.8 %collective-permute-start.15 = (bf16[2,384,128]{2,1,0:T(8,128)(2,1)}, bf16[2,384,128]{2,1,0:T(8,128)(2,1)}, u32[]{:S(2)}, u32[]{:S(2)}) collective-permute-start(bf16[2,384,128]{2,1,0:T(8,128)(2,1)} %slice.59), channel_id=1, source_target_pairs={{0,3},{1,0},{2,1},{3,2},{4,7},{5,4},{6,5},{7,6},{8,11},{9,8},{10,9... | collective-permute-start | bytes 589832 | tf_op jit(solution)/shard_map/ppermute | solution.py:32
  109.1 10.6 %collective-permute-start.16 = (bf16[192,384]{1,0:T(8,128)(2,1)}, bf16[192,384]{1,0:T(8,128)(2,1)S(1)}, u32[]{:S(2)}, u32[]{:S(2)}) collective-permute-start(bf16[192,384]{1,0:T(8,128)(2,1)} %get-tuple-element.38), channel_id=1, source_target_pairs={{0,128},{1,129},{2,130},{3,131},{4,132},{5,133},{6,134},{7,135},{8... | collective-permute-start | bytes 442376 | tf_op jit(solution)/shard_map/ppermute | solution.py:32
  120.7 5.5 %collective-permute-start.19 = (bf16[96,384]{1,0:T(8,128)(2,1)S(1)}, bf16[96,384]{1,0:T(8,128)(2,1)S(1)}, u32[]{:S(2)}, u32[]{:S(2)}) collective-permute-start(bf16[96,384]{1,0:T(8,128)(2,1)S(1)} %get-tuple-element.74), channel_id=1, source_target_pairs={{0,1},{1,2},{2,3},{3,0},{4,5},{5,6},{6,7},{7,4},{8,9},{9,10},{10,1... | collective-permute-start | bytes 221192 | tf_op jit(solution)/shard_map/ppermute | solution.py:32
  120.8 9.5 %collective-permute-start.26 = (bf16[96,384]{1,0:T(8,128)(2,1)S(1)}, bf16[96,384]{1,0:T(8,128)(2,1)S(1)}, u32[]{:S(2)}, u32[]{:S(2)}) collective-permute-start(bf16[96,384]{1,0:T(8,128)(2,1)S(1)} %get-tuple-element.73), channel_id=1, source_target_pairs={{0,4},{1,5},{2,6},{3,7},{4,8},{5,9},{6,10},{7,11},{8,12},{9,13},{1... | collective-permute-start | bytes 221192 | tf_op jit(solution)/shard_map/ppermute | solution.py:32
  120.9 9.4 %collective-permute-start.18 = (bf16[96,384]{1,0:T(8,128)(2,1)S(1)}, bf16[96,384]{1,0:T(8,128)(2,1)S(1)}, u32[]{:S(2)}, u32[]{:S(2)}) collective-permute-start(bf16[96,384]{1,0:T(8,128)(2,1)S(1)} %get-tuple-element.74), channel_id=1, source_target_pairs={{0,3},{1,0},{2,1},{3,2},{4,7},{5,4},{6,5},{7,6},{8,11},{9,8},{10,9... | collective-permute-start | bytes 221192 | tf_op jit(solution)/shard_map/ppermute | solution.py:32
  126.3 5.1 %collective-permute-start.20 = (bf16[96,384]{1,0:T(8,128)(2,1)S(1)}, bf16[96,384]{1,0:T(8,128)(2,1)S(1)}, u32[]{:S(2)}, u32[]{:S(2)}) collective-permute-start(bf16[96,384]{1,0:T(8,128)(2,1)S(1)} %collective-permute-done.19), channel_id=1, source_target_pairs={{0,1},{1,2},{2,3},{3,0},{4,5},{5,6},{6,7},{7,4},{8,9},{9,10},{10,1... | collective-permute-start | bytes 221192 | tf_op jit(solution)/shard_map/ppermute | solution.py:32
  126.3 8.7 %collective-permute-start.25 = (bf16[96,384]{1,0:T(8,128)(2,1)S(1)}, bf16[96,384]{1,0:T(8,128)(2,1)S(1)}, u32[]{:S(2)}, u32[]{:S(2)}) collective-permute-start(bf16[96,384]{1,0:T(8,128)(2,1)S(1)} %get-tuple-element.73), channel_id=1, source_target_pairs={{0,12},{1,13},{2,14},{3,15},{4,0},{5,1},{6,2},{7,3},{8,4},{9,5},{1... | collective-permute-start | bytes 221192 | tf_op jit(solution)/shard_map/ppermute | solution.py:32
  130.3 28.2 %collective-permute-start.17 = (bf16[768,384]{1,0:T(8,128)(2,1)}, bf16[768,384]{1,0:T(8,128)(2,1)S(1)}, u32[]{:S(2)}, u32[]{:S(2)}) collective-permute-start(bf16[768,384]{1,0:T(8,128)(2,1)} %get-tuple-element.39.mine_ref), channel_id=1, source_target_pairs={{0,128},{1,129},{2,130},{3,131},{4,132},{5,133},{6,134},{7,135},{8... | collective-permute-start | bytes 1769480 | tf_op jit(solution)/shard_map/ppermute | solution.py:32
  130.3 5.7 %collective-permute-start.27 = (bf16[96,384]{1,0:T(8,128)(2,1)S(1)}, bf16[96,384]{1,0:T(8,128)(2,1)S(1)}, u32[]{:S(2)}, u32[]{:S(2)}) collective-permute-start(bf16[96,384]{1,0:T(8,128)(2,1)S(1)} %collective-permute-done.26), channel_id=1, source_target_pairs={{0,4},{1,5},{2,6},{3,7},{4,8},{5,9},{6,10},{7,11},{8,12},{9,13},{1... | collective-permute-start | bytes 221192 | tf_op jit(solution)/shard_map/ppermute | solution.py:32
  131.4 10.4 %collective-permute-start.22 = (bf16[4,96,384]{2,1,0:T(8,128)(2,1)S(1)}, bf16[4,96,384]{2,1,0:T(8,128)(2,1)S(1)}, u32[]{:S(2)}, u32[]{:S(2)}) collective-permute-start(bf16[4,96,384]{2,1,0:T(8,128)(2,1)S(1)} %pad_maximum_fusion.2.refs_0_), channel_id=1, source_target_pairs={{0,4},{1,5},{2,6},{3,7},{4,8},{5,9},{6,10},{7,11},{8,12},{9,13},{1... | collective-permute-start | bytes 884744 | tf_op jit(solution)/shard_map/ppermute | solution.py:32
  131.5 10.7 %collective-permute-start.21 = (bf16[4,96,384]{2,1,0:T(8,128)(2,1)S(1)}, bf16[4,96,384]{2,1,0:T(8,128)(2,1)S(1)}, u32[]{:S(2)}, u32[]{:S(2)}) collective-permute-start(bf16[4,96,384]{2,1,0:T(8,128)(2,1)S(1)} %pad_maximum_fusion.2.refs_0_), channel_id=1, source_target_pairs={{0,12},{1,13},{2,14},{3,15},{4,0},{5,1},{6,2},{7,3},{8,4},{9,5},{1... | collective-permute-start | bytes 884744 | tf_op jit(solution)/shard_map/ppermute | solution.py:32
  136.1 8.9 %collective-permute-start.29 = (bf16[4,96,384]{2,1,0:T(8,128)(2,1)S(1)}, bf16[4,96,384]{2,1,0:T(8,128)(2,1)S(1)}, u32[]{:S(2)}, u32[]{:S(2)}) collective-permute-start(bf16[4,96,384]{2,1,0:T(8,128)(2,1)S(1)} %pad_maximum_fusion.3.refs_5_), channel_id=1, source_target_pairs={{0,1},{1,2},{2,3},{3,0},{4,5},{5,6},{6,7},{7,4},{8,9},{9,10},{10,1... | collective-permute-start | bytes 884744 | tf_op jit(solution)/shard_map/ppermute | solution.py:32
  138.2 9.4 %collective-permute-start.28 = (bf16[4,96,384]{2,1,0:T(8,128)(2,1)S(1)}, bf16[4,96,384]{2,1,0:T(8,128)(2,1)S(1)}, u32[]{:S(2)}, u32[]{:S(2)}) collective-permute-start(bf16[4,96,384]{2,1,0:T(8,128)(2,1)S(1)} %pad_maximum_fusion.3.refs_5_), channel_id=1, source_target_pairs={{0,3},{1,0},{2,1},{3,2},{4,7},{5,4},{6,5},{7,6},{8,11},{9,8},{10,9... | collective-permute-start | bytes 884744 | tf_op jit(solution)/shard_map/ppermute | solution.py:32
  141.9 6.0 %collective-permute-start.23 = (bf16[2,96,384]{2,1,0:T(8,128)(2,1)S(1)}, bf16[2,96,384]{2,1,0:T(8,128)(2,1)S(1)}, u32[]{:S(2)}, u32[]{:S(2)}) collective-permute-start(bf16[2,96,384]{2,1,0:T(8,128)(2,1)S(1)} %slice.61), channel_id=1, source_target_pairs={{0,4},{1,5},{2,6},{3,7},{4,8},{5,9},{6,10},{7,11},{8,12},{9,13},{1... | collective-permute-start | bytes 442376 | tf_op jit(solution)/shard_map/ppermute | solution.py:32
  142.3 5.6 %collective-permute-start.24 = (bf16[2,96,384]{2,1,0:T(8,128)(2,1)S(1)}, bf16[2,96,384]{2,1,0:T(8,128)(2,1)S(1)}, u32[]{:S(2)}, u32[]{:S(2)}) collective-permute-start(bf16[2,96,384]{2,1,0:T(8,128)(2,1)S(1)} %slice.62), channel_id=1, source_target_pairs={{0,12},{1,13},{2,14},{3,15},{4,0},{5,1},{6,2},{7,3},{8,4},{9,5},{1... | collective-permute-start | bytes 442376 | tf_op jit(solution)/shard_map/ppermute | solution.py:32
  145.0 5.6 %collective-permute-start.30 = (bf16[2,96,384]{2,1,0:T(8,128)(2,1)S(1)}, bf16[2,96,384]{2,1,0:T(8,128)(2,1)S(1)}, u32[]{:S(2)}, u32[]{:S(2)}) collective-permute-start(bf16[2,96,384]{2,1,0:T(8,128)(2,1)S(1)} %slice.64), channel_id=1, source_target_pairs={{0,1},{1,2},{2,3},{3,0},{4,5},{5,6},{6,7},{7,4},{8,9},{9,10},{10,1... | collective-permute-start | bytes 442376 | tf_op jit(solution)/shard_map/ppermute | solution.py:32
  147.7 5.2 %collective-permute-start.31 = (bf16[2,96,384]{2,1,0:T(8,128)(2,1)S(1)}, bf16[2,96,384]{2,1,0:T(8,128)(2,1)S(1)}, u32[]{:S(2)}, u32[]{:S(2)}) collective-permute-start(bf16[2,96,384]{2,1,0:T(8,128)(2,1)S(1)} %slice.65), channel_id=1, source_target_pairs={{0,3},{1,0},{2,1},{3,2},{4,7},{5,4},{6,5},{7,6},{8,11},{9,8},{10,9... | collective-permute-start | bytes 442376 | tf_op jit(solution)/shard_map/ppermute | solution.py:32
  158.6 7.1 %collective-permute-start.33 = (bf16[256,384]{1,0:T(8,128)(2,1)}, bf16[256,384]{1,0:T(8,128)(2,1)S(1)}, u32[]{:S(2)}, u32[]{:S(2)}) collective-permute-start(bf16[256,384]{1,0:T(8,128)(2,1)} %get-tuple-element.47.refs_0_), channel_id=1, source_target_pairs={{0,32},{1,33},{2,34},{3,35},{4,36},{5,37},{6,38},{7,39},{8,40},{9,... | collective-permute-start | bytes 589832 | tf_op jit(solution)/shard_map/ppermute | solution.py:32
  161.8 6.2 %collective-permute-start.32 = (bf16[256,384]{1,0:T(8,128)(2,1)}, bf16[256,384]{1,0:T(8,128)(2,1)S(1)}, u32[]{:S(2)}, u32[]{:S(2)}) collective-permute-start(bf16[256,384]{1,0:T(8,128)(2,1)} %get-tuple-element.47.refs_0_), channel_id=1, source_target_pairs={{0,96},{1,97},{2,98},{3,99},{4,100},{5,101},{6,102},{7,103},{8,104... | collective-permute-start | bytes 589832 | tf_op jit(solution)/shard_map/ppermute | solution.py:32
  165.7 8.1 %collective-permute-start.34 = (bf16[128,384]{1,0:T(8,128)(2,1)S(1)}, bf16[128,384]{1,0:T(8,128)(2,1)S(1)}, u32[]{:S(2)}, u32[]{:S(2)}) collective-permute-start(bf16[128,384]{1,0:T(8,128)(2,1)S(1)} %slice.66), channel_id=1, source_target_pairs={{0,32},{1,33},{2,34},{3,35},{4,36},{5,37},{6,38},{7,39},{8,40},{9,... | collective-permute-start | bytes 294920 | tf_op jit(solution)/shard_map/ppermute | solution.py:32
  168.0 9.7 %collective-permute-start.35 = (bf16[128,384]{1,0:T(8,128)(2,1)S(1)}, bf16[128,384]{1,0:T(8,128)(2,1)S(1)}, u32[]{:S(2)}, u32[]{:S(2)}) collective-permute-start(bf16[128,384]{1,0:T(8,128)(2,1)S(1)} %slice.67), channel_id=1, source_target_pairs={{0,96},{1,97},{2,98},{3,99},{4,100},{5,101},{6,102},{7,103},{8,104... | collective-permute-start | bytes 294920 | tf_op jit(solution)/shard_map/ppermute | solution.py:32
  177.7 10.5 %collective-permute-start.36 = (bf16[256,384]{1,0:T(8,128)(2,1)}, bf16[256,384]{1,0:T(8,128)(2,1)S(1)}, u32[]{:S(2)}, u32[]{:S(2)}) collective-permute-start(bf16[256,384]{1,0:T(8,128)(2,1)} %get-tuple-element.47.refs_0_), channel_id=1, source_target_pairs={{0,16},{1,17},{2,18},{3,19},{4,20},{5,21},{6,22},{7,23},{8,24},{9,... | collective-permute-start | bytes 589832 | tf_op jit(solution)/shard_map/ppermute | solution.py:32
  186.2 2.0 collective-permute-start.37
  186.2 2.0 %collective-permute-start.40 = (bf16[256,384]{1,0:T(8,128)(2,1)S(1)}, bf16[256,384]{1,0:T(8,128)(2,1)S(1)}, u32[]{:S(2)}, u32[]{:S(2)}) collective-permute-start(bf16[256,384]{1,0:T(8,128)(2,1)S(1)} %collective-permute-done.33.refs_4_), channel_id=1, source_target_pairs={{0,16},{1,17},{2,18},{3,19},{4,20},{5,21},{6,22},{7,23},{8,24},{9,... | collective-permute-start | bytes 589832 | tf_op jit(solution)/shard_map/ppermute | solution.py:32
  186.7 1.4 collective-permute-start.38
  186.7 1.5 collective-permute-start.39
  (25 other events, 266.2 us)
Sparse Core Ops, SparseCore 0:
  16.5 86.2 all-gather.4
  105.2 74.6 all-gather.6
where the time goes:
time: 203 us; the launch traced here: 202 us
  starting transfers between devices  102 us (50%)
  waiting for transfers between devices  45.9 us (23%)
  Pallas kernels  22.4 us (11%)
  between operations  14.6 us (7%)
  local copies, waits for them, and re-layouts  12.4 us (6%)
  other arithmetic  4.94 us (2%)
    ppermute x42, starting transfers between devices, permute(): return lax.ppermute(array, AXES, pairs)  102 us
    ppermute x42, waiting for transfers between devices, permute(): return lax.ppermute(array, AXES, pairs)  36.5 us
    pallas_call x5, Pallas kernels, call(): pl.pallas_call(kernel, in_specs=[smem] * len(scalars) + [anywhere] * len(...  22.4 us
    all_gather x1, waiting for transfers between devices, per_device(): right = lax.all_gather(right_here, 'row', axis=0, tiled=False)  9.34 us
    unnamed x64, local copies, waits for them, and re-layouts  8.55 us
  transfers between devices with their start and end apart: 44, of which 20 were waited for; matrix products, arithmetic and copies ran while one was open for 5% of the time, Pallas kernels for 7%

commit v1 on v0

--- a/solution.py
+++ b/solution.py
@@ -334,8 +334,6 @@
         (turned, root_slots, offdiag_slots, slots, part_slots, my_picks, other_picks)
     )
     root_parts = plane_gather(turned[:384], turned[384:])
-    child_here = lax.optimization_barrier((child_here, root_parts))[0]
-    child_left = lax.all_gather(child_here, "col", axis=0, tiled=False)
 
     partial, theirs, mine = call(
         root_kernel,
@@ -351,6 +349,8 @@
         ],
         (other_picks, my_picks),
     )
+    child_here = lax.optimization_barrier((child_here, partial))[0]
+    child_left = lax.all_gather(child_here, "col", axis=0, tiled=False)
     theirs = permute(theirs, other_half)
     picked = (mine.astype(jnp.float32) + theirs.astype(jnp.float32)).astype(bf16)
     late = lax.optimization_barrier((partial, picked))[0]

time: 203 us -> 200 us (0.985)
  starting transfers between devices: 102 us -> 97 us
    ppermute x42, starting transfers between devices: 102 us -> 96.9 us  [permute(): return lax.ppermute(array, AXES, pairs)]
  transfers between devices with their start and end apart: 44 -> 44, of which waited for: 20 -> 17; matrix products, arithmetic and copies ran while one was open for 5% -> 5% of each run, Pallas kernels for 7% -> 7%
where the time goes in v1:
time: 200 us; the launch traced here: 199 us
  starting transfers between devices  97 us (48%)
  waiting for transfers between devices  46.9 us (23%)
  Pallas kernels  22.4 us (11%)
  between operations  14.7 us (7%)
  local copies, waits for them, and re-layouts  13.2 us (7%)
  other arithmetic  4.98 us (2%)
    ppermute x42, starting transfers between devices, permute(): return lax.ppermute(array, AXES, pairs)  96.9 us
    ppermute x42, waiting for transfers between devices, permute(): return lax.ppermute(array, AXES, pairs)  36.6 us
    pallas_call x5, Pallas kernels, call(): pl.pallas_call(kernel, in_specs=[smem] * len(scalars) + [anywhere] * len(...  22.4 us
    all_gather x1, waiting for transfers between devices, per_device(): right = lax.all_gather(right_here, 'row', axis=0, tiled=False)  10.2 us
    unnamed x64, local copies, waits for them, and re-layouts  9.3 us
  transfers between devices with their start and end apart: 44, of which 17 were waited for; matrix products, arithmetic and copies ran while one was open for 5% of the time, Pallas kernels for 7%

profile of v1, /device:TPU:1, one launch (start us, length us, event | category | flops | bytes accessed | tf_op | source)
XLA Modules:
  0.0 199.1 jit_solution(15631592195978086608)
XLA Ops:
  7.2 1.3 copy.30
  8.5 1.6 copy.29
  10.1 1.7 copy.28
  11.8 1.2 copy.13
  13.8 2.6 %shard_map.85 = (bf16[768,128]{1,0:T(8,128)(2,1)}, bf16[1536,128]{1,0:T(8,128)(2,1)}, bf16[2304,128]{1,0:T(8,128)(2,1)}) custom-call(bf16[384,384]{1,0:T(8,128)(2,1)} %bitcast.58, f32[3,128]{1,0:T(4,128)} %bitcast.77, bf16[512,256]{1,0:T(8,128)(2,1)} %bitcast.59, f32[4,128]{1,0:T(4,128)} %bitcast.78, bf16[384,256]{1,0:T(8,128)(2,1)} %bitcast.60), custom_call_target="tpu_custom_call" | custom-call | tf_op jit(solution)/shard_map/pallas_call | solution.py:279
  17.0 1.4 reduce.9
  19.7 2.6 %collective-permute-start.1 = (s32[576,1]{1,0:T(8,128)S(1)}, s32[576,1]{1,0:T(8,128)S(1)}, u32[]{:S(2)}, u32[]{:S(2)}) collective-permute-start(s32[576,1]{1,0:T(8,128)S(1)} %copy.14), channel_id=1, source_target_pairs={{0,128},{1,129},{2,130},{3,131},{4,132},{5,133},{6,134},{7,135},{8... | collective-permute-start | bytes 6920 | tf_op jit(solution)/shard_map/ppermute | solution.py:32
  22.2 3.9 %collective-permute-start = (bf16[768,128]{1,0:T(8,128)(2,1)}, bf16[768,128]{1,0:T(8,128)(2,1)S(1)}, u32[]{:S(2)}, u32[]{:S(2)}) collective-permute-start(bf16[768,128]{1,0:T(8,128)(2,1)} %get-tuple-element.29), channel_id=1, source_target_pairs={{0,0},{1,17},{2,38},{3,55},{4,68},{5,85},{6,98},{7,115},{8,8},{9,2... | collective-permute-start | bytes 589832 | tf_op jit(solution)/shard_map/ppermute | solution.py:32
  29.2 1.0 collective-permute-start.3
  30.2 12.9 %collective-permute-start.10 = (bf16[384,128]{1,0:T(8,128)(2,1)S(1)}, bf16[384,128]{1,0:T(8,128)(2,1)S(1)}, u32[]{:S(2)}, u32[]{:S(2)}) collective-permute-start(bf16[384,128]{1,0:T(8,128)(2,1)S(1)} %get-tuple-element.69), channel_id=1, source_target_pairs={{0,4},{1,5},{2,6},{3,7},{4,8},{5,9},{6,10},{7,11},{8,12},{9,13},{1... | collective-permute-start | bytes 294920 | tf_op jit(solution)/shard_map/ppermute | solution.py:32
  43.1 15.4 %collective-permute-start.2 = (bf16[384,128]{1,0:T(8,128)(2,1)S(1)}, bf16[384,128]{1,0:T(8,128)(2,1)S(1)}, u32[]{:S(2)}, u32[]{:S(2)}) collective-permute-start(bf16[384,128]{1,0:T(8,128)(2,1)S(1)} %get-tuple-element.70), channel_id=1, source_target_pairs={{0,3},{1,0},{2,1},{3,2},{4,7},{5,4},{6,5},{7,6},{8,11},{9,8},{10,9... | collective-permute-start | bytes 294920 | tf_op jit(solution)/shard_map/ppermute | solution.py:32
  58.4 3.9 %collective-permute-start.9 = (bf16[384,128]{1,0:T(8,128)(2,1)S(1)}, bf16[384,128]{1,0:T(8,128)(2,1)S(1)}, u32[]{:S(2)}, u32[]{:S(2)}) collective-permute-start(bf16[384,128]{1,0:T(8,128)(2,1)S(1)} %get-tuple-element.69), channel_id=1, source_target_pairs={{0,12},{1,13},{2,14},{3,15},{4,0},{5,1},{6,2},{7,3},{8,4},{9,5},{1... | collective-permute-start | bytes 294920 | tf_op jit(solution)/shard_map/ppermute | solution.py:32
  62.4 1.1 collective-permute-done.4
  63.6 2.3 %collective-permute-start.6 = (bf16[4,384,128]{2,1,0:T(8,128)(2,1)S(1)}, bf16[4,384,128]{2,1,0:T(8,128)(2,1)S(1)}, u32[]{:S(2)}, u32[]{:S(2)}) collective-permute-start(bf16[4,384,128]{2,1,0:T(8,128)(2,1)S(1)} %pad_maximum_fusion.refs_0_), channel_id=1, source_target_pairs={{0,4},{1,5},{2,6},{3,7},{4,8},{5,9},{6,10},{7,11},{8,12},{9,13},{1... | collective-permute-start | bytes 1179656 | tf_op jit(solution)/shard_map/ppermute | solution.py:32
  65.9 1.8 collective-permute-start.5
  68.0 2.7 %collective-permute-start.12 = (bf16[4,384,128]{2,1,0:T(8,128)(2,1)S(1)}, bf16[4,384,128]{2,1,0:T(8,128)(2,1)S(1)}, u32[]{:S(2)}, u32[]{:S(2)}) collective-permute-start(bf16[4,384,128]{2,1,0:T(8,128)(2,1)S(1)} %pad_maximum_fusion.1.refs_5_), channel_id=1, source_target_pairs={{0,3},{1,0},{2,1},{3,2},{4,7},{5,4},{6,5},{7,6},{8,11},{9,8},{10,9... | collective-permute-start | bytes 1179656 | tf_op jit(solution)/shard_map/ppermute | solution.py:32
  70.6 5.0 %collective-permute-start.41 = (bf16[1536,128]{1,0:T(8,128)(2,1)}, bf16[1536,128]{1,0:T(8,128)(2,1)S(1)}, u32[]{:S(2)}, u32[]{:S(2)}) collective-permute-start(bf16[1536,128]{1,0:T(8,128)(2,1)} %get-tuple-element.53), channel_id=1, source_target_pairs={{0,0},{1,17},{2,38},{3,55},{4,68},{5,85},{6,98},{7,115},{8,8},{9,2... | collective-permute-start | bytes 1179656 | tf_op jit(solution)/shard_map/ppermute | solution.py:32
  75.6 1.4 collective-permute-done.6.refs_4_
  77.0 1.3 collective-permute-start.7
  78.3 2.0 %collective-permute-start.8 = (bf16[2,384,128]{2,1,0:T(8,128)(2,1)S(1)}, bf16[2,384,128]{2,1,0:T(8,128)(2,1)}, u32[]{:S(2)}, u32[]{:S(2)}) collective-permute-start(bf16[2,384,128]{2,1,0:T(8,128)(2,1)S(1)} %slice.57), channel_id=1, source_target_pairs={{0,12},{1,13},{2,14},{3,15},{4,0},{5,1},{6,2},{7,3},{8,4},{9,5},{1... | collective-permute-start | bytes 589832 | tf_op jit(solution)/shard_map/ppermute | solution.py:32
  81.8 2.7 %collective-permute-start.15 = (bf16[2,384,128]{2,1,0:T(8,128)(2,1)}, bf16[2,384,128]{2,1,0:T(8,128)(2,1)}, u32[]{:S(2)}, u32[]{:S(2)}) collective-permute-start(bf16[2,384,128]{2,1,0:T(8,128)(2,1)} %slice.59), channel_id=1, source_target_pairs={{0,3},{1,0},{2,1},{3,2},{4,7},{5,4},{6,5},{7,6},{8,11},{9,8},{10,9... | collective-permute-start | bytes 589832 | tf_op jit(solution)/shard_map/ppermute | solution.py:32
  84.4 0.9 copy.15.refs_12_
  85.3 5.8 %collective-permute-done.7.refs_2_ = bf16[2,384,128]{2,1,0:T(8,128)(2,1)} collective-permute-done((bf16[2,384,128]{2,1,0:T(8,128)(2,1)S(1)}, bf16[2,384,128]{2,1,0:T(8,128)(2,1)}, u32[]{:S(2)}, u32[]{:S(2)}) %collective-permute-start.7) | collective-permute-done | bytes 196640 | tf_op jit(solution)/shard_map/ppermute | solution.py:32
  91.1 1.4 collective-permute-done.15.refs_8_
  92.5 10.2 %all-gather.5.cloned.1.call-done = bf16[18432,128]{1,0:T(8,128)(2,1)} async-done(((bf16[2304,128]{1,0:T(8,128)(2,1)}), bf16[18432,128]{1,0:T(8,128)(2,1)}) %all-gather.5.cloned.1.call-update) | async-done | bytes 4718608 | tf_op jit(solution)/shard_map/all_gather | solution.py:308
  102.8 6.3 %shard_map.86 = (bf16[768,384]{1,0:T(8,128)(2,1)}, bf16[192,384]{1,0:T(8,128)(2,1)}, bf16[192,384]{1,0:T(8,128)(2,1)}) custom-call(s32[16]{0:T(128)} %multiply_add_fusion.4.slot_one, s32[16]{0:T(128)} %get-tuple-element.31.slot_two, bf16[4,384,128]{2,1,0:T(8,128)(2,1)} %copy-done, bf16[4,384,128]{2,1,0:T(8,128)(2,1)} %copy-done.5, ...), custom_call_target="tpu_custom_call" | custom-call | tf_op jit(solution)/shard_map/pallas_call | solution.py:279
  109.9 6.2 %collective-permute-start.16 = (bf16[192,384]{1,0:T(8,128)(2,1)}, bf16[192,384]{1,0:T(8,128)(2,1)S(1)}, u32[]{:S(2)}, u32[]{:S(2)}) collective-permute-start(bf16[192,384]{1,0:T(8,128)(2,1)} %get-tuple-element.38), channel_id=1, source_target_pairs={{0,128},{1,129},{2,130},{3,131},{4,132},{5,133},{6,134},{7,135},{8... | collective-permute-start | bytes 442376 | tf_op jit(solution)/shard_map/ppermute | solution.py:32
  116.1 3.6 %collective-permute-done.16 = bf16[192,384]{1,0:T(8,128)(2,1)S(1)} collective-permute-done((bf16[192,384]{1,0:T(8,128)(2,1)}, bf16[192,384]{1,0:T(8,128)(2,1)S(1)}, u32[]{:S(2)}, u32[]{:S(2)}) %collective-permute-start.16) | collective-permute-done | bytes 147488 | tf_op jit(solution)/shard_map/ppermute | solution.py:32
  119.7 1.0 add_convert_fusion
  120.8 3.8 %collective-permute-start.18 = (bf16[96,384]{1,0:T(8,128)(2,1)S(1)}, bf16[96,384]{1,0:T(8,128)(2,1)S(1)}, u32[]{:S(2)}, u32[]{:S(2)}) collective-permute-start(bf16[96,384]{1,0:T(8,128)(2,1)S(1)} %get-tuple-element.74), channel_id=1, source_target_pairs={{0,3},{1,0},{2,1},{3,2},{4,7},{5,4},{6,5},{7,6},{8,11},{9,8},{10,9... | collective-permute-start | bytes 221192 | tf_op jit(solution)/shard_map/ppermute | solution.py:32
  124.6 1.6 collective-permute-done.19
  126.2 1.0 collective-permute-start.25
  127.2 1.1 collective-permute-start.17
  128.8 3.1 %collective-permute-done.20 = bf16[96,384]{1,0:T(8,128)(2,1)S(1)} collective-permute-done((bf16[96,384]{1,0:T(8,128)(2,1)S(1)}, bf16[96,384]{1,0:T(8,128)(2,1)S(1)}, u32[]{:S(2)}, u32[]{:S(2)}) %collective-permute-start.20) | collective-permute-done | bytes 73760 | tf_op jit(solution)/shard_map/ppermute | solution.py:32
  132.1 2.7 %collective-permute-start.21 = (bf16[4,96,384]{2,1,0:T(8,128)(2,1)S(1)}, bf16[4,96,384]{2,1,0:T(8,128)(2,1)S(1)}, u32[]{:S(2)}, u32[]{:S(2)}) collective-permute-start(bf16[4,96,384]{2,1,0:T(8,128)(2,1)S(1)} %pad_maximum_fusion.2.refs_0_), channel_id=1, source_target_pairs={{0,12},{1,13},{2,14},{3,15},{4,0},{5,1},{6,2},{7,3},{8,4},{9,5},{1... | collective-permute-start | bytes 884744 | tf_op jit(solution)/shard_map/ppermute | solution.py:32
  134.9 2.7 %collective-permute-start.28 = (bf16[4,96,384]{2,1,0:T(8,128)(2,1)S(1)}, bf16[4,96,384]{2,1,0:T(8,128)(2,1)S(1)}, u32[]{:S(2)}, u32[]{:S(2)}) collective-permute-start(bf16[4,96,384]{2,1,0:T(8,128)(2,1)S(1)} %pad_maximum_fusion.3.refs_5_), channel_id=1, source_target_pairs={{0,3},{1,0},{2,1},{3,2},{4,7},{5,4},{6,5},{7,6},{8,11},{9,8},{10,9... | collective-permute-start | bytes 884744 | tf_op jit(solution)/shard_map/ppermute | solution.py:32
  137.6 7.3 %collective-permute-done.22.refs_4_ = bf16[4,96,384]{2,1,0:T(8,128)(2,1)S(1)} collective-permute-done((bf16[4,96,384]{2,1,0:T(8,128)(2,1)S(1)}, bf16[4,96,384]{2,1,0:T(8,128)(2,1)S(1)}, u32[]{:S(2)}, u32[]{:S(2)}) %collective-permute-start.22) | collective-permute-done | bytes 294944 | tf_op jit(solution)/shard_map/ppermute | solution.py:32
  145.3 2.7 %collective-permute-start.24 = (bf16[2,96,384]{2,1,0:T(8,128)(2,1)S(1)}, bf16[2,96,384]{2,1,0:T(8,128)(2,1)S(1)}, u32[]{:S(2)}, u32[]{:S(2)}) collective-permute-start(bf16[2,96,384]{2,1,0:T(8,128)(2,1)S(1)} %slice.62), channel_id=1, source_target_pairs={{0,12},{1,13},{2,14},{3,15},{4,0},{5,1},{6,2},{7,3},{8,4},{9,5},{1... | collective-permute-start | bytes 442376 | tf_op jit(solution)/shard_map/ppermute | solution.py:32
  148.2 2.7 %collective-permute-start.31 = (bf16[2,96,384]{2,1,0:T(8,128)(2,1)S(1)}, bf16[2,96,384]{2,1,0:T(8,128)(2,1)S(1)}, u32[]{:S(2)}, u32[]{:S(2)}) collective-permute-start(bf16[2,96,384]{2,1,0:T(8,128)(2,1)S(1)} %slice.65), channel_id=1, source_target_pairs={{0,3},{1,0},{2,1},{3,2},{4,7},{5,4},{6,5},{7,6},{8,11},{9,8},{10,9... | collective-permute-start | bytes 442376 | tf_op jit(solution)/shard_map/ppermute | solution.py:32
  150.9 2.4 %collective-permute-done.30.refs_7_ = bf16[2,96,384]{2,1,0:T(8,128)(2,1)S(1)} collective-permute-done((bf16[2,96,384]{2,1,0:T(8,128)(2,1)S(1)}, bf16[2,96,384]{2,1,0:T(8,128)(2,1)S(1)}, u32[]{:S(2)}, u32[]{:S(2)}) %collective-permute-start.30) | collective-permute-done | bytes 147488 | tf_op jit(solution)/shard_map/ppermute | solution.py:32
  153.3 1.7 collective-permute-done.31.refs_8_
  155.7 4.9 %shard_map.88 = (f32[768,128]{1,0:T(8,128)}, bf16[256,384]{1,0:T(8,128)(2,1)}) custom-call(s32[16]{0:T(128)} %multiply_add_fusion.2.slot_one, s32[16]{0:T(128)} %get-tuple-element.41.slot_two, bf16[4,96,384]{2,1,0:T(8,128)(2,1)} %copy-done.2, bf16[4,96,384]{2,1,0:T(8,128)(2,1)} %copy-done.9, bf16[2,96,384]{2,1,0:T(8,128)(2,1)} %copy-done.20, ...), custom_call_target="tpu_custom_call" | custom-call | tf_op jit(solution)/shard_map/pallas_call | solution.py:279
  160.8 3.6 %collective-permute-start.32 = (bf16[256,384]{1,0:T(8,128)(2,1)}, bf16[256,384]{1,0:T(8,128)(2,1)S(1)}, u32[]{:S(2)}, u32[]{:S(2)}) collective-permute-start(bf16[256,384]{1,0:T(8,128)(2,1)} %get-tuple-element.47.refs_0_), channel_id=1, source_target_pairs={{0,96},{1,97},{2,98},{3,99},{4,100},{5,101},{6,102},{7,103},{8,104... | collective-permute-start | bytes 589832 | tf_op jit(solution)/shard_map/ppermute | solution.py:32
  164.3 5.3 %collective-permute-done.33.refs_4_ = bf16[256,384]{1,0:T(8,128)(2,1)S(1)} collective-permute-done((bf16[256,384]{1,0:T(8,128)(2,1)}, bf16[256,384]{1,0:T(8,128)(2,1)S(1)}, u32[]{:S(2)}, u32[]{:S(2)}) %collective-permute-start.33) | collective-permute-done | bytes 196640 | tf_op jit(solution)/shard_map/ppermute | solution.py:32
  169.8 3.6 %collective-permute-start.35 = (bf16[128,384]{1,0:T(8,128)(2,1)S(1)}, bf16[128,384]{1,0:T(8,128)(2,1)S(1)}, u32[]{:S(2)}, u32[]{:S(2)}) collective-permute-start(bf16[128,384]{1,0:T(8,128)(2,1)S(1)} %slice.67), channel_id=1, source_target_pairs={{0,96},{1,97},{2,98},{3,99},{4,100},{5,101},{6,102},{7,103},{8,104... | collective-permute-start | bytes 294920 | tf_op jit(solution)/shard_map/ppermute | solution.py:32
  173.4 2.4 %shard_map.87 = f32[2304,128]{1,0:T(8,128)} custom-call(bf16[768,384]{1,0:T(8,128)(2,1)} %get-tuple-element.39.mine_ref, bf16[768,384]{1,0:T(8,128)(2,1)} %copy-done.12), custom_call_target="tpu_custom_call" | custom-call | tf_op jit(solution)/shard_map/pallas_call | solution.py:279
  176.2 7.0 %collective-permute-start.36 = (bf16[256,384]{1,0:T(8,128)(2,1)}, bf16[256,384]{1,0:T(8,128)(2,1)S(1)}, u32[]{:S(2)}, u32[]{:S(2)}) collective-permute-start(bf16[256,384]{1,0:T(8,128)(2,1)} %get-tuple-element.47.refs_0_), channel_id=1, source_target_pairs={{0,16},{1,17},{2,18},{3,19},{4,20},{5,21},{6,22},{7,23},{8,24},{9,... | collective-permute-start | bytes 589832 | tf_op jit(solution)/shard_map/ppermute | solution.py:32
  186.0 6.2 %shard_map.89 = f32[1024,128]{1,0:T(8,128)} custom-call(s32[16]{0:T(128)} %copy-done.28, s32[8]{0:T(128)} %multiply_add_fusion.part_slots, bf16[256,384]{1,0:T(8,128)(2,1)} %get-tuple-element.47.refs_0_, bf16[256,384]{1,0:T(8,128)(2,1)} %copy-done.14, bf16[128,384]{1,0:T(8,128)(2,1)} %copy-done.24, bf16[128,384]{1,0:T(8,128)(2,1)} %copy-done.25, ...), custom_call_target="tpu_custom_call" | custom-call | tf_op jit(solution)/shard_map/pallas_call | solution.py:279
  (152 shorter events, 13.6 us)
Async XLA Ops:
  7.2 95.6 %all-gather.5.cloned.1.call-start = ((), (), s32[]{:S(2)}) async-start(), calls=%async_computation | async-start | bytes 5308416 | tf_op jit(solution)/shard_map/all_gather | solution.py:308
  16.4 168.9 %all-gather.7.cloned.1.call-start = ((), (), s32[]{:S(2)}) async-start(), calls=%async_computation.1 | async-start | bytes 6684672 | tf_op jit(solution)/shard_map/all_gather | solution.py:353
  19.7 9.1 %collective-permute-start.1 = (s32[576,1]{1,0:T(8,128)S(1)}, s32[576,1]{1,0:T(8,128)S(1)}, u32[]{:S(2)}, u32[]{:S(2)}) collective-permute-start(s32[576,1]{1,0:T(8,128)S(1)} %copy.14), channel_id=1, source_target_pairs={{0,128},{1,129},{2,130},{3,131},{4,132},{5,133},{6,134},{7,135},{8... | collective-permute-start | bytes 6920 | tf_op jit(solution)/shard_map/ppermute | solution.py:32
  22.2 6.9 %collective-permute-start = (bf16[768,128]{1,0:T(8,128)(2,1)}, bf16[768,128]{1,0:T(8,128)(2,1)S(1)}, u32[]{:S(2)}, u32[]{:S(2)}) collective-permute-start(bf16[768,128]{1,0:T(8,128)(2,1)} %get-tuple-element.29), channel_id=1, source_target_pairs={{0,0},{1,17},{2,38},{3,55},{4,68},{5,85},{6,98},{7,115},{8,8},{9,2... | collective-permute-start | bytes 589832 | tf_op jit(solution)/shard_map/ppermute | solution.py:32
  26.5 82.7 %copy-start.28 = (s32[16]{0:T(128)}, s32[16]{0:T(128)S(1)}, u32[]{:S(2)}) copy-start(s32[16]{0:T(128)S(1)} %add.180.slots) | copy-start | bytes 196
  28.7 74.1 %copy-start.16 = (s32[576,1]{1,0:T(8,128)}, s32[576,1]{1,0:T(8,128)S(1)}, u32[]{:S(2)}) copy-start(s32[576,1]{1,0:T(8,128)S(1)} %collective-permute-done.1.refs_11_) | copy-start | bytes 6916
  29.2 29.3 %collective-permute-start.3 = (bf16[384,128]{1,0:T(8,128)(2,1)S(1)}, bf16[384,128]{1,0:T(8,128)(2,1)S(1)}, u32[]{:S(2)}, u32[]{:S(2)}) collective-permute-start(bf16[384,128]{1,0:T(8,128)(2,1)S(1)} %get-tuple-element.70), channel_id=1, source_target_pairs={{0,1},{1,2},{2,3},{3,0},{4,5},{5,6},{6,7},{7,4},{8,9},{9,10},{10,1... | collective-permute-start | bytes 294920 | tf_op jit(solution)/shard_map/ppermute | solution.py:32
  30.2 32.2 %collective-permute-start.10 = (bf16[384,128]{1,0:T(8,128)(2,1)S(1)}, bf16[384,128]{1,0:T(8,128)(2,1)S(1)}, u32[]{:S(2)}, u32[]{:S(2)}) collective-permute-start(bf16[384,128]{1,0:T(8,128)(2,1)S(1)} %get-tuple-element.69), channel_id=1, source_target_pairs={{0,4},{1,5},{2,6},{3,7},{4,8},{5,9},{6,10},{7,11},{8,12},{9,13},{1... | collective-permute-start | bytes 294920 | tf_op jit(solution)/shard_map/ppermute | solution.py:32
  43.1 19.3 %collective-permute-start.2 = (bf16[384,128]{1,0:T(8,128)(2,1)S(1)}, bf16[384,128]{1,0:T(8,128)(2,1)S(1)}, u32[]{:S(2)}, u32[]{:S(2)}) collective-permute-start(bf16[384,128]{1,0:T(8,128)(2,1)S(1)} %get-tuple-element.70), channel_id=1, source_target_pairs={{0,3},{1,0},{2,1},{3,2},{4,7},{5,4},{6,5},{7,6},{8,11},{9,8},{10,9... | collective-permute-start | bytes 294920 | tf_op jit(solution)/shard_map/ppermute | solution.py:32
  58.4 5.1 %collective-permute-start.4 = (bf16[384,128]{1,0:T(8,128)(2,1)S(1)}, bf16[384,128]{1,0:T(8,128)(2,1)S(1)}, u32[]{:S(2)}, u32[]{:S(2)}) collective-permute-start(bf16[384,128]{1,0:T(8,128)(2,1)S(1)} %collective-permute-done.3), channel_id=1, source_target_pairs={{0,1},{1,2},{2,3},{3,0},{4,5},{5,6},{6,7},{7,4},{8,9},{9,10},{10,1... | collective-permute-start | bytes 294920 | tf_op jit(solution)/shard_map/ppermute | solution.py:32
  58.4 9.3 %collective-permute-start.9 = (bf16[384,128]{1,0:T(8,128)(2,1)S(1)}, bf16[384,128]{1,0:T(8,128)(2,1)S(1)}, u32[]{:S(2)}, u32[]{:S(2)}) collective-permute-start(bf16[384,128]{1,0:T(8,128)(2,1)S(1)} %get-tuple-element.69), channel_id=1, source_target_pairs={{0,12},{1,13},{2,14},{3,15},{4,0},{5,1},{6,2},{7,3},{8,4},{9,5},{1... | collective-permute-start | bytes 294920 | tf_op jit(solution)/shard_map/ppermute | solution.py:32
  62.4 5.4 %collective-permute-start.11 = (bf16[384,128]{1,0:T(8,128)(2,1)S(1)}, bf16[384,128]{1,0:T(8,128)(2,1)S(1)}, u32[]{:S(2)}, u32[]{:S(2)}) collective-permute-start(bf16[384,128]{1,0:T(8,128)(2,1)S(1)} %collective-permute-done.10), channel_id=1, source_target_pairs={{0,4},{1,5},{2,6},{3,7},{4,8},{5,9},{6,10},{7,11},{8,12},{9,13},{1... | collective-permute-start | bytes 294920 | tf_op jit(solution)/shard_map/ppermute | solution.py:32
  63.6 39.2 %copy-start = (bf16[4,384,128]{2,1,0:T(8,128)(2,1)}, bf16[4,384,128]{2,1,0:T(8,128)(2,1)S(1)}, u32[]{:S(2)}) copy-start(bf16[4,384,128]{2,1,0:T(8,128)(2,1)S(1)} %pad_maximum_fusion.refs_0_) | copy-start | bytes 1179652
  63.6 13.4 %collective-permute-start.6 = (bf16[4,384,128]{2,1,0:T(8,128)(2,1)S(1)}, bf16[4,384,128]{2,1,0:T(8,128)(2,1)S(1)}, u32[]{:S(2)}, u32[]{:S(2)}) collective-permute-start(bf16[4,384,128]{2,1,0:T(8,128)(2,1)S(1)} %pad_maximum_fusion.refs_0_), channel_id=1, source_target_pairs={{0,4},{1,5},{2,6},{3,7},{4,8},{5,9},{6,10},{7,11},{8,12},{9,13},{1... | collective-permute-start | bytes 1179656 | tf_op jit(solution)/shard_map/ppermute | solution.py:32
  65.9 12.3 %collective-permute-start.5 = (bf16[4,384,128]{2,1,0:T(8,128)(2,1)S(1)}, bf16[4,384,128]{2,1,0:T(8,128)(2,1)S(1)}, u32[]{:S(2)}, u32[]{:S(2)}) collective-permute-start(bf16[4,384,128]{2,1,0:T(8,128)(2,1)S(1)} %pad_maximum_fusion.refs_0_), channel_id=1, source_target_pairs={{0,12},{1,13},{2,14},{3,15},{4,0},{5,1},{6,2},{7,3},{8,4},{9,5},{1... | collective-permute-start | bytes 1179656 | tf_op jit(solution)/shard_map/ppermute | solution.py:32
  67.9 34.9 %copy-start.1 = (bf16[4,384,128]{2,1,0:T(8,128)(2,1)}, bf16[4,384,128]{2,1,0:T(8,128)(2,1)S(1)}, u32[]{:S(2)}) copy-start(bf16[4,384,128]{2,1,0:T(8,128)(2,1)S(1)} %pad_maximum_fusion.1.refs_5_) | copy-start | bytes 1179652
  67.9 12.4 %collective-permute-start.13 = (bf16[4,384,128]{2,1,0:T(8,128)(2,1)S(1)}, bf16[4,384,128]{2,1,0:T(8,128)(2,1)S(1)}, u32[]{:S(2)}, u32[]{:S(2)}) collective-permute-start(bf16[4,384,128]{2,1,0:T(8,128)(2,1)S(1)} %pad_maximum_fusion.1.refs_5_), channel_id=1, source_target_pairs={{0,1},{1,2},{2,3},{3,0},{4,5},{5,6},{6,7},{7,4},{8,9},{9,10},{10,1... | collective-permute-start | bytes 1179656 | tf_op jit(solution)/shard_map/ppermute | solution.py:32
  68.0 13.1 %collective-permute-start.12 = (bf16[4,384,128]{2,1,0:T(8,128)(2,1)S(1)}, bf16[4,384,128]{2,1,0:T(8,128)(2,1)S(1)}, u32[]{:S(2)}, u32[]{:S(2)}) collective-permute-start(bf16[4,384,128]{2,1,0:T(8,128)(2,1)S(1)} %pad_maximum_fusion.1.refs_5_), channel_id=1, source_target_pairs={{0,3},{1,0},{2,1},{3,2},{4,7},{5,4},{6,5},{7,6},{8,11},{9,8},{10,9... | collective-permute-start | bytes 1179656 | tf_op jit(solution)/shard_map/ppermute | solution.py:32
  70.6 38.5 %collective-permute-start.41 = (bf16[1536,128]{1,0:T(8,128)(2,1)}, bf16[1536,128]{1,0:T(8,128)(2,1)S(1)}, u32[]{:S(2)}, u32[]{:S(2)}) collective-permute-start(bf16[1536,128]{1,0:T(8,128)(2,1)} %get-tuple-element.53), channel_id=1, source_target_pairs={{0,0},{1,17},{2,38},{3,55},{4,68},{5,85},{6,98},{7,115},{8,8},{9,2... | collective-permute-start | bytes 1179656 | tf_op jit(solution)/shard_map/ppermute | solution.py:32
  77.0 14.2 %collective-permute-start.7 = (bf16[2,384,128]{2,1,0:T(8,128)(2,1)S(1)}, bf16[2,384,128]{2,1,0:T(8,128)(2,1)}, u32[]{:S(2)}, u32[]{:S(2)}) collective-permute-start(bf16[2,384,128]{2,1,0:T(8,128)(2,1)S(1)} %slice.56), channel_id=1, source_target_pairs={{0,4},{1,5},{2,6},{3,7},{4,8},{5,9},{6,10},{7,11},{8,12},{9,13},{1... | collective-permute-start | bytes 589832 | tf_op jit(solution)/shard_map/ppermute | solution.py:32
  78.3 12.9 %collective-permute-start.8 = (bf16[2,384,128]{2,1,0:T(8,128)(2,1)S(1)}, bf16[2,384,128]{2,1,0:T(8,128)(2,1)}, u32[]{:S(2)}, u32[]{:S(2)}) collective-permute-start(bf16[2,384,128]{2,1,0:T(8,128)(2,1)S(1)} %slice.57), channel_id=1, source_target_pairs={{0,12},{1,13},{2,14},{3,15},{4,0},{5,1},{6,2},{7,3},{8,4},{9,5},{1... | collective-permute-start | bytes 589832 | tf_op jit(solution)/shard_map/ppermute | solution.py:32
  81.0 10.1 %collective-permute-start.14 = (bf16[2,384,128]{2,1,0:T(8,128)(2,1)}, bf16[2,384,128]{2,1,0:T(8,128)(2,1)}, u32[]{:S(2)}, u32[]{:S(2)}) collective-permute-start(bf16[2,384,128]{2,1,0:T(8,128)(2,1)} %slice.58), channel_id=1, source_target_pairs={{0,1},{1,2},{2,3},{3,0},{4,5},{5,6},{6,7},{7,4},{8,9},{9,10},{10,1... | collective-permute-start | bytes 589832 | tf_op jit(solution)/shard_map/ppermute | solution.py:32
  81.8 10.8 %collective-permute-start.15 = (bf16[2,384,128]{2,1,0:T(8,128)(2,1)}, bf16[2,384,128]{2,1,0:T(8,128)(2,1)}, u32[]{:S(2)}, u32[]{:S(2)}) collective-permute-start(bf16[2,384,128]{2,1,0:T(8,128)(2,1)} %slice.59), channel_id=1, source_target_pairs={{0,3},{1,0},{2,1},{3,2},{4,7},{5,4},{6,5},{7,6},{8,11},{9,8},{10,9... | collective-permute-start | bytes 589832 | tf_op jit(solution)/shard_map/ppermute | solution.py:32
  109.9 9.7 %collective-permute-start.16 = (bf16[192,384]{1,0:T(8,128)(2,1)}, bf16[192,384]{1,0:T(8,128)(2,1)S(1)}, u32[]{:S(2)}, u32[]{:S(2)}) collective-permute-start(bf16[192,384]{1,0:T(8,128)(2,1)} %get-tuple-element.38), channel_id=1, source_target_pairs={{0,128},{1,129},{2,130},{3,131},{4,132},{5,133},{6,134},{7,135},{8... | collective-permute-start | bytes 442376 | tf_op jit(solution)/shard_map/ppermute | solution.py:32
  120.7 5.5 %collective-permute-start.19 = (bf16[96,384]{1,0:T(8,128)(2,1)S(1)}, bf16[96,384]{1,0:T(8,128)(2,1)S(1)}, u32[]{:S(2)}, u32[]{:S(2)}) collective-permute-start(bf16[96,384]{1,0:T(8,128)(2,1)S(1)} %get-tuple-element.74), channel_id=1, source_target_pairs={{0,1},{1,2},{2,3},{3,0},{4,5},{5,6},{6,7},{7,4},{8,9},{9,10},{10,1... | collective-permute-start | bytes 221192 | tf_op jit(solution)/shard_map/ppermute | solution.py:32
  120.8 7.6 %collective-permute-start.26 = (bf16[96,384]{1,0:T(8,128)(2,1)S(1)}, bf16[96,384]{1,0:T(8,128)(2,1)S(1)}, u32[]{:S(2)}, u32[]{:S(2)}) collective-permute-start(bf16[96,384]{1,0:T(8,128)(2,1)S(1)} %get-tuple-element.73), channel_id=1, source_target_pairs={{0,4},{1,5},{2,6},{3,7},{4,8},{5,9},{6,10},{7,11},{8,12},{9,13},{1... | collective-permute-start | bytes 221192 | tf_op jit(solution)/shard_map/ppermute | solution.py:32
  120.8 8.0 %collective-permute-start.18 = (bf16[96,384]{1,0:T(8,128)(2,1)S(1)}, bf16[96,384]{1,0:T(8,128)(2,1)S(1)}, u32[]{:S(2)}, u32[]{:S(2)}) collective-permute-start(bf16[96,384]{1,0:T(8,128)(2,1)S(1)} %get-tuple-element.74), channel_id=1, source_target_pairs={{0,3},{1,0},{2,1},{3,2},{4,7},{5,4},{6,5},{7,6},{8,11},{9,8},{10,9... | collective-permute-start | bytes 221192 | tf_op jit(solution)/shard_map/ppermute | solution.py:32
  126.2 5.8 %collective-permute-start.20 = (bf16[96,384]{1,0:T(8,128)(2,1)S(1)}, bf16[96,384]{1,0:T(8,128)(2,1)S(1)}, u32[]{:S(2)}, u32[]{:S(2)}) collective-permute-start(bf16[96,384]{1,0:T(8,128)(2,1)S(1)} %collective-permute-done.19), channel_id=1, source_target_pairs={{0,1},{1,2},{2,3},{3,0},{4,5},{5,6},{6,7},{7,4},{8,9},{9,10},{10,1... | collective-permute-start | bytes 221192 | tf_op jit(solution)/shard_map/ppermute | solution.py:32
  126.2 8.6 %collective-permute-start.25 = (bf16[96,384]{1,0:T(8,128)(2,1)S(1)}, bf16[96,384]{1,0:T(8,128)(2,1)S(1)}, u32[]{:S(2)}, u32[]{:S(2)}) collective-permute-start(bf16[96,384]{1,0:T(8,128)(2,1)S(1)} %get-tuple-element.73), channel_id=1, source_target_pairs={{0,12},{1,13},{2,14},{3,15},{4,0},{5,1},{6,2},{7,3},{8,4},{9,5},{1... | collective-permute-start | bytes 221192 | tf_op jit(solution)/shard_map/ppermute | solution.py:32
  127.2 33.4 %collective-permute-start.17 = (bf16[768,384]{1,0:T(8,128)(2,1)}, bf16[768,384]{1,0:T(8,128)(2,1)S(1)}, u32[]{:S(2)}, u32[]{:S(2)}) collective-permute-start(bf16[768,384]{1,0:T(8,128)(2,1)} %get-tuple-element.39.mine_ref), channel_id=1, source_target_pairs={{0,128},{1,129},{2,130},{3,131},{4,132},{5,133},{6,134},{7,135},{8... | collective-permute-start | bytes 1769480 | tf_op jit(solution)/shard_map/ppermute | solution.py:32
  128.4 6.4 %collective-permute-start.27 = (bf16[96,384]{1,0:T(8,128)(2,1)S(1)}, bf16[96,384]{1,0:T(8,128)(2,1)S(1)}, u32[]{:S(2)}, u32[]{:S(2)}) collective-permute-start(bf16[96,384]{1,0:T(8,128)(2,1)S(1)} %collective-permute-done.26), channel_id=1, source_target_pairs={{0,4},{1,5},{2,6},{3,7},{4,8},{5,9},{6,10},{7,11},{8,12},{9,13},{1... | collective-permute-start | bytes 221192 | tf_op jit(solution)/shard_map/ppermute | solution.py:32
  132.0 12.9 %collective-permute-start.22 = (bf16[4,96,384]{2,1,0:T(8,128)(2,1)S(1)}, bf16[4,96,384]{2,1,0:T(8,128)(2,1)S(1)}, u32[]{:S(2)}, u32[]{:S(2)}) collective-permute-start(bf16[4,96,384]{2,1,0:T(8,128)(2,1)S(1)} %pad_maximum_fusion.2.refs_0_), channel_id=1, source_target_pairs={{0,4},{1,5},{2,6},{3,7},{4,8},{5,9},{6,10},{7,11},{8,12},{9,13},{1... | collective-permute-start | bytes 884744 | tf_op jit(solution)/shard_map/ppermute | solution.py:32
  132.1 13.1 %collective-permute-start.21 = (bf16[4,96,384]{2,1,0:T(8,128)(2,1)S(1)}, bf16[4,96,384]{2,1,0:T(8,128)(2,1)S(1)}, u32[]{:S(2)}, u32[]{:S(2)}) collective-permute-start(bf16[4,96,384]{2,1,0:T(8,128)(2,1)S(1)} %pad_maximum_fusion.2.refs_0_), channel_id=1, source_target_pairs={{0,12},{1,13},{2,14},{3,15},{4,0},{5,1},{6,2},{7,3},{8,4},{9,5},{1... | collective-permute-start | bytes 884744 | tf_op jit(solution)/shard_map/ppermute | solution.py:32
  134.9 13.2 %collective-permute-start.29 = (bf16[4,96,384]{2,1,0:T(8,128)(2,1)S(1)}, bf16[4,96,384]{2,1,0:T(8,128)(2,1)S(1)}, u32[]{:S(2)}, u32[]{:S(2)}) collective-permute-start(bf16[4,96,384]{2,1,0:T(8,128)(2,1)S(1)} %pad_maximum_fusion.3.refs_5_), channel_id=1, source_target_pairs={{0,1},{1,2},{2,3},{3,0},{4,5},{5,6},{6,7},{7,4},{8,9},{9,10},{10,1... | collective-permute-start | bytes 884744 | tf_op jit(solution)/shard_map/ppermute | solution.py:32
  134.9 13.2 %collective-permute-start.28 = (bf16[4,96,384]{2,1,0:T(8,128)(2,1)S(1)}, bf16[4,96,384]{2,1,0:T(8,128)(2,1)S(1)}, u32[]{:S(2)}, u32[]{:S(2)}) collective-permute-start(bf16[4,96,384]{2,1,0:T(8,128)(2,1)S(1)} %pad_maximum_fusion.3.refs_5_), channel_id=1, source_target_pairs={{0,3},{1,0},{2,1},{3,2},{4,7},{5,4},{6,5},{7,6},{8,11},{9,8},{10,9... | collective-permute-start | bytes 884744 | tf_op jit(solution)/shard_map/ppermute | solution.py:32
  145.0 6.0 %collective-permute-start.23 = (bf16[2,96,384]{2,1,0:T(8,128)(2,1)S(1)}, bf16[2,96,384]{2,1,0:T(8,128)(2,1)S(1)}, u32[]{:S(2)}, u32[]{:S(2)}) collective-permute-start(bf16[2,96,384]{2,1,0:T(8,128)(2,1)S(1)} %slice.61), channel_id=1, source_target_pairs={{0,4},{1,5},{2,6},{3,7},{4,8},{5,9},{6,10},{7,11},{8,12},{9,13},{1... | collective-permute-start | bytes 442376 | tf_op jit(solution)/shard_map/ppermute | solution.py:32
  145.3 5.6 %collective-permute-start.24 = (bf16[2,96,384]{2,1,0:T(8,128)(2,1)S(1)}, bf16[2,96,384]{2,1,0:T(8,128)(2,1)S(1)}, u32[]{:S(2)}, u32[]{:S(2)}) collective-permute-start(bf16[2,96,384]{2,1,0:T(8,128)(2,1)S(1)} %slice.62), channel_id=1, source_target_pairs={{0,12},{1,13},{2,14},{3,15},{4,0},{5,1},{6,2},{7,3},{8,4},{9,5},{1... | collective-permute-start | bytes 442376 | tf_op jit(solution)/shard_map/ppermute | solution.py:32
  148.1 5.3 %collective-permute-start.30 = (bf16[2,96,384]{2,1,0:T(8,128)(2,1)S(1)}, bf16[2,96,384]{2,1,0:T(8,128)(2,1)S(1)}, u32[]{:S(2)}, u32[]{:S(2)}) collective-permute-start(bf16[2,96,384]{2,1,0:T(8,128)(2,1)S(1)} %slice.64), channel_id=1, source_target_pairs={{0,1},{1,2},{2,3},{3,0},{4,5},{5,6},{6,7},{7,4},{8,9},{9,10},{10,1... | collective-permute-start | bytes 442376 | tf_op jit(solution)/shard_map/ppermute | solution.py:32
  148.2 6.8 %collective-permute-start.31 = (bf16[2,96,384]{2,1,0:T(8,128)(2,1)S(1)}, bf16[2,96,384]{2,1,0:T(8,128)(2,1)S(1)}, u32[]{:S(2)}, u32[]{:S(2)}) collective-permute-start(bf16[2,96,384]{2,1,0:T(8,128)(2,1)S(1)} %slice.65), channel_id=1, source_target_pairs={{0,3},{1,0},{2,1},{3,2},{4,7},{5,4},{6,5},{7,6},{8,11},{9,8},{10,9... | collective-permute-start | bytes 442376 | tf_op jit(solution)/shard_map/ppermute | solution.py:32
  160.7 9.0 %collective-permute-start.33 = (bf16[256,384]{1,0:T(8,128)(2,1)}, bf16[256,384]{1,0:T(8,128)(2,1)S(1)}, u32[]{:S(2)}, u32[]{:S(2)}) collective-permute-start(bf16[256,384]{1,0:T(8,128)(2,1)} %get-tuple-element.47.refs_0_), channel_id=1, source_target_pairs={{0,32},{1,33},{2,34},{3,35},{4,36},{5,37},{6,38},{7,39},{8,40},{9,... | collective-permute-start | bytes 589832 | tf_op jit(solution)/shard_map/ppermute | solution.py:32
  160.8 9.0 %collective-permute-start.32 = (bf16[256,384]{1,0:T(8,128)(2,1)}, bf16[256,384]{1,0:T(8,128)(2,1)S(1)}, u32[]{:S(2)}, u32[]{:S(2)}) collective-permute-start(bf16[256,384]{1,0:T(8,128)(2,1)} %get-tuple-element.47.refs_0_), channel_id=1, source_target_pairs={{0,96},{1,97},{2,98},{3,99},{4,100},{5,101},{6,102},{7,103},{8,104... | collective-permute-start | bytes 589832 | tf_op jit(solution)/shard_map/ppermute | solution.py:32
  169.7 6.5 %collective-permute-start.34 = (bf16[128,384]{1,0:T(8,128)(2,1)S(1)}, bf16[128,384]{1,0:T(8,128)(2,1)S(1)}, u32[]{:S(2)}, u32[]{:S(2)}) collective-permute-start(bf16[128,384]{1,0:T(8,128)(2,1)S(1)} %slice.66), channel_id=1, source_target_pairs={{0,32},{1,33},{2,34},{3,35},{4,36},{5,37},{6,38},{7,39},{8,40},{9,... | collective-permute-start | bytes 294920 | tf_op jit(solution)/shard_map/ppermute | solution.py:32
  169.8 6.4 %collective-permute-start.35 = (bf16[128,384]{1,0:T(8,128)(2,1)S(1)}, bf16[128,384]{1,0:T(8,128)(2,1)S(1)}, u32[]{:S(2)}, u32[]{:S(2)}) collective-permute-start(bf16[128,384]{1,0:T(8,128)(2,1)S(1)} %slice.67), channel_id=1, source_target_pairs={{0,96},{1,97},{2,98},{3,99},{4,100},{5,101},{6,102},{7,103},{8,104... | collective-permute-start | bytes 294920 | tf_op jit(solution)/shard_map/ppermute | solution.py:32
  176.2 9.0 %collective-permute-start.36 = (bf16[256,384]{1,0:T(8,128)(2,1)}, bf16[256,384]{1,0:T(8,128)(2,1)S(1)}, u32[]{:S(2)}, u32[]{:S(2)}) collective-permute-start(bf16[256,384]{1,0:T(8,128)(2,1)} %get-tuple-element.47.refs_0_), channel_id=1, source_target_pairs={{0,16},{1,17},{2,18},{3,19},{4,20},{5,21},{6,22},{7,23},{8,24},{9,... | collective-permute-start | bytes 589832 | tf_op jit(solution)/shard_map/ppermute | solution.py:32
  183.2 2.0 %collective-permute-start.37 = (bf16[256,384]{1,0:T(8,128)(2,1)S(1)}, bf16[256,384]{1,0:T(8,128)(2,1)S(1)}, u32[]{:S(2)}, u32[]{:S(2)}) collective-permute-start(bf16[256,384]{1,0:T(8,128)(2,1)S(1)} %collective-permute-done.32.refs_1_), channel_id=1, source_target_pairs={{0,16},{1,17},{2,18},{3,19},{4,20},{5,21},{6,22},{7,23},{8,24},{9,... | collective-permute-start | bytes 589832 | tf_op jit(solution)/shard_map/ppermute | solution.py:32
  183.2 2.0 %collective-permute-start.40 = (bf16[256,384]{1,0:T(8,128)(2,1)S(1)}, bf16[256,384]{1,0:T(8,128)(2,1)S(1)}, u32[]{:S(2)}, u32[]{:S(2)}) collective-permute-start(bf16[256,384]{1,0:T(8,128)(2,1)S(1)} %collective-permute-done.33.refs_4_), channel_id=1, source_target_pairs={{0,16},{1,17},{2,18},{3,19},{4,20},{5,21},{6,22},{7,23},{8,24},{9,... | collective-permute-start | bytes 589832 | tf_op jit(solution)/shard_map/ppermute | solution.py:32
  183.7 1.4 collective-permute-start.38
  183.7 1.5 collective-permute-start.39
  (25 other events, 248.8 us)
Sparse Core Ops, SparseCore 0:
  16.5 86.2 all-gather.4
  110.1 71.3 all-gather.6

commit v2 on v1

--- a/solution.py
+++ b/solution.py
@@ -53,7 +53,7 @@
 
 
 def mixed(r, p):
-    return (r // 2 - p // 2) % SIDE * 2 + (r ^ p) % 2
+    return (r // 2 - p // 2 + r % 2 * 2) % SIDE * 2 + (r ^ p) % 2
 
 
 def transposed_place(h, r, q):

time: 200 us -> 201 us (level)
  waiting for transfers between devices: 46.9 us -> 56 us
  starting transfers between devices: 97 us -> 88.6 us
    ppermute x42, waiting for transfers between devices: 36.6 us -> 47.6 us  [permute(): return lax.ppermute(array, AXES, pairs)]
    ppermute x42, starting transfers between devices: 96.9 us -> 88.5 us  [permute(): return lax.ppermute(array, AXES, pairs)]
where the time goes in v2:
time: 201 us; the launch traced here: 200 us
  starting transfers between devices  88.6 us (44%)
  waiting for transfers between devices  56 us (28%)
  Pallas kernels  22.4 us (11%)
  between operations  14.6 us (7%)
  local copies, waits for them, and re-layouts  13.6 us (7%)
  other arithmetic  4.98 us (2%)
    ppermute x42, starting transfers between devices, permute(): return lax.ppermute(array, AXES, pairs)  88.5 us
    ppermute x42, waiting for transfers between devices, permute(): return lax.ppermute(array, AXES, pairs)  47.6 us
    pallas_call x5, Pallas kernels, call(): pl.pallas_call(kernel, in_specs=[smem] * len(scalars) + [anywhere] * len(...  22.4 us
    unnamed x64, local copies, waits for them, and re-layouts  9.71 us
    all_gather x1, waiting for transfers between devices, per_device(): right = lax.all_gather(right_here, 'row', axis=0, tiled=False)  8.34 us
  transfers between devices with their start and end apart: 44, of which 17 were waited for; matrix products, arithmetic and copies ran while one was open for 5% of the time, Pallas kernels for 7%

profile of v2, /device:TPU:1, one launch (start us, length us, event | category | flops | bytes accessed | tf_op | source)
XLA Modules:
  0.0 200.3 jit_solution(11834909469344788713)
XLA Ops:
  7.2 1.3 copy.30
  8.5 1.6 copy.29
  10.1 1.7 copy.28
  11.8 1.2 copy.13
  13.8 2.6 %shard_map.85 = (bf16[768,128]{1,0:T(8,128)(2,1)}, bf16[1536,128]{1,0:T(8,128)(2,1)}, bf16[2304,128]{1,0:T(8,128)(2,1)}) custom-call(bf16[384,384]{1,0:T(8,128)(2,1)} %bitcast.58, f32[3,128]{1,0:T(4,128)} %bitcast.77, bf16[512,256]{1,0:T(8,128)(2,1)} %bitcast.59, f32[4,128]{1,0:T(4,128)} %bitcast.78, bf16[384,256]{1,0:T(8,128)(2,1)} %bitcast.60), custom_call_target="tpu_custom_call" | custom-call | tf_op jit(solution)/shard_map/pallas_call | solution.py:279
  17.0 1.4 reduce.9
  19.7 2.6 %collective-permute-start.1 = (s32[576,1]{1,0:T(8,128)S(1)}, s32[576,1]{1,0:T(8,128)S(1)}, u32[]{:S(2)}, u32[]{:S(2)}) collective-permute-start(s32[576,1]{1,0:T(8,128)S(1)} %copy.14), channel_id=1, source_target_pairs={{0,128},{1,129},{2,130},{3,131},{4,132},{5,133},{6,134},{7,135},{8... | collective-permute-start | bytes 6920 | tf_op jit(solution)/shard_map/ppermute | solution.py:32
  22.2 5.0 %collective-permute-start = (bf16[768,128]{1,0:T(8,128)(2,1)}, bf16[768,128]{1,0:T(8,128)(2,1)S(1)}, u32[]{:S(2)}, u32[]{:S(2)}) collective-permute-start(bf16[768,128]{1,0:T(8,128)(2,1)} %get-tuple-element.29), channel_id=1, source_target_pairs={{0,0},{1,17},{2,38},{3,55},{4,68},{5,85},{6,98},{7,115},{8,8},{9,2... | collective-permute-start | bytes 589832 | tf_op jit(solution)/shard_map/ppermute | solution.py:32
  29.7 9.8 %collective-permute-done = bf16[768,128]{1,0:T(8,128)(2,1)S(1)} collective-permute-done((bf16[768,128]{1,0:T(8,128)(2,1)}, bf16[768,128]{1,0:T(8,128)(2,1)S(1)}, u32[]{:S(2)}, u32[]{:S(2)}) %collective-permute-start) | collective-permute-done | bytes 196640 | tf_op jit(solution)/shard_map/ppermute | solution.py:32
  39.7 3.3 %collective-permute-start.10 = (bf16[384,128]{1,0:T(8,128)(2,1)S(1)}, bf16[384,128]{1,0:T(8,128)(2,1)S(1)}, u32[]{:S(2)}, u32[]{:S(2)}) collective-permute-start(bf16[384,128]{1,0:T(8,128)(2,1)S(1)} %get-tuple-element.69), channel_id=1, source_target_pairs={{0,4},{1,5},{2,6},{3,7},{4,8},{5,9},{6,10},{7,11},{8,12},{9,13},{1... | collective-permute-start | bytes 294920 | tf_op jit(solution)/shard_map/ppermute | solution.py:32
  43.0 15.4 %collective-permute-start.2 = (bf16[384,128]{1,0:T(8,128)(2,1)S(1)}, bf16[384,128]{1,0:T(8,128)(2,1)S(1)}, u32[]{:S(2)}, u32[]{:S(2)}) collective-permute-start(bf16[384,128]{1,0:T(8,128)(2,1)S(1)} %get-tuple-element.70), channel_id=1, source_target_pairs={{0,3},{1,0},{2,1},{3,2},{4,7},{5,4},{6,5},{7,6},{8,11},{9,8},{10,9... | collective-permute-start | bytes 294920 | tf_op jit(solution)/shard_map/ppermute | solution.py:32
  58.4 4.0 %collective-permute-start.9 = (bf16[384,128]{1,0:T(8,128)(2,1)S(1)}, bf16[384,128]{1,0:T(8,128)(2,1)S(1)}, u32[]{:S(2)}, u32[]{:S(2)}) collective-permute-start(bf16[384,128]{1,0:T(8,128)(2,1)S(1)} %get-tuple-element.69), channel_id=1, source_target_pairs={{0,12},{1,13},{2,14},{3,15},{4,0},{5,1},{6,2},{7,3},{8,4},{9,5},{1... | collective-permute-start | bytes 294920 | tf_op jit(solution)/shard_map/ppermute | solution.py:32
  62.4 1.1 collective-permute-done.4
  63.6 2.3 %collective-permute-start.6 = (bf16[4,384,128]{2,1,0:T(8,128)(2,1)S(1)}, bf16[4,384,128]{2,1,0:T(8,128)(2,1)S(1)}, u32[]{:S(2)}, u32[]{:S(2)}) collective-permute-start(bf16[4,384,128]{2,1,0:T(8,128)(2,1)S(1)} %pad_maximum_fusion.refs_0_), channel_id=1, source_target_pairs={{0,4},{1,5},{2,6},{3,7},{4,8},{5,9},{6,10},{7,11},{8,12},{9,13},{1... | collective-permute-start | bytes 1179656 | tf_op jit(solution)/shard_map/ppermute | solution.py:32
  65.9 1.8 collective-permute-start.5
  67.9 2.7 %collective-permute-start.12 = (bf16[4,384,128]{2,1,0:T(8,128)(2,1)S(1)}, bf16[4,384,128]{2,1,0:T(8,128)(2,1)S(1)}, u32[]{:S(2)}, u32[]{:S(2)}) collective-permute-start(bf16[4,384,128]{2,1,0:T(8,128)(2,1)S(1)} %pad_maximum_fusion.1.refs_5_), channel_id=1, source_target_pairs={{0,3},{1,0},{2,1},{3,2},{4,7},{5,4},{6,5},{7,6},{8,11},{9,8},{10,9... | collective-permute-start | bytes 1179656 | tf_op jit(solution)/shard_map/ppermute | solution.py:32
  70.5 6.3 %collective-permute-start.41 = (bf16[1536,128]{1,0:T(8,128)(2,1)}, bf16[1536,128]{1,0:T(8,128)(2,1)S(1)}, u32[]{:S(2)}, u32[]{:S(2)}) collective-permute-start(bf16[1536,128]{1,0:T(8,128)(2,1)} %get-tuple-element.53), channel_id=1, source_target_pairs={{0,0},{1,17},{2,38},{3,55},{4,68},{5,85},{6,98},{7,115},{8,8},{9,2... | collective-permute-start | bytes 1179656 | tf_op jit(solution)/shard_map/ppermute | solution.py:32
  76.9 3.8 %collective-permute-start.7 = (bf16[2,384,128]{2,1,0:T(8,128)(2,1)S(1)}, bf16[2,384,128]{2,1,0:T(8,128)(2,1)}, u32[]{:S(2)}, u32[]{:S(2)}) collective-permute-start(bf16[2,384,128]{2,1,0:T(8,128)(2,1)S(1)} %slice.56), channel_id=1, source_target_pairs={{0,4},{1,5},{2,6},{3,7},{4,8},{5,9},{6,10},{7,11},{8,12},{9,13},{1... | collective-permute-start | bytes 589832 | tf_op jit(solution)/shard_map/ppermute | solution.py:32
  82.3 2.7 %collective-permute-start.15 = (bf16[2,384,128]{2,1,0:T(8,128)(2,1)}, bf16[2,384,128]{2,1,0:T(8,128)(2,1)}, u32[]{:S(2)}, u32[]{:S(2)}) collective-permute-start(bf16[2,384,128]{2,1,0:T(8,128)(2,1)} %slice.59), channel_id=1, source_target_pairs={{0,3},{1,0},{2,1},{3,2},{4,7},{5,4},{6,5},{7,6},{8,11},{9,8},{10,9... | collective-permute-start | bytes 589832 | tf_op jit(solution)/shard_map/ppermute | solution.py:32
  85.8 8.0 %collective-permute-done.14.refs_7_ = bf16[2,384,128]{2,1,0:T(8,128)(2,1)} collective-permute-done((bf16[2,384,128]{2,1,0:T(8,128)(2,1)}, bf16[2,384,128]{2,1,0:T(8,128)(2,1)}, u32[]{:S(2)}, u32[]{:S(2)}) %collective-permute-start.14) | collective-permute-done | bytes 196640 | tf_op jit(solution)/shard_map/ppermute | solution.py:32
  93.8 8.3 %all-gather.5.cloned.1.call-done = bf16[18432,128]{1,0:T(8,128)(2,1)} async-done(((bf16[2304,128]{1,0:T(8,128)(2,1)}), bf16[18432,128]{1,0:T(8,128)(2,1)}) %all-gather.5.cloned.1.call-update) | async-done | bytes 4718608 | tf_op jit(solution)/shard_map/all_gather | solution.py:308
  102.2 6.3 %shard_map.86 = (bf16[768,384]{1,0:T(8,128)(2,1)}, bf16[192,384]{1,0:T(8,128)(2,1)}, bf16[192,384]{1,0:T(8,128)(2,1)}) custom-call(s32[16]{0:T(128)} %multiply_add_fusion.3.slot_one, s32[16]{0:T(128)} %get-tuple-element.31.slot_two, bf16[4,384,128]{2,1,0:T(8,128)(2,1)} %copy-done, bf16[4,384,128]{2,1,0:T(8,128)(2,1)} %copy-done.5, ...), custom_call_target="tpu_custom_call" | custom-call | tf_op jit(solution)/shard_map/pallas_call | solution.py:279
  109.4 4.2 %collective-permute-done.16 = bf16[192,384]{1,0:T(8,128)(2,1)S(1)} collective-permute-done((bf16[192,384]{1,0:T(8,128)(2,1)}, bf16[192,384]{1,0:T(8,128)(2,1)S(1)}, u32[]{:S(2)}, u32[]{:S(2)}) %collective-permute-start.16) | collective-permute-done | bytes 147488 | tf_op jit(solution)/shard_map/ppermute | solution.py:32
  113.6 1.0 add_convert_fusion
  114.6 4.0 %collective-permute-start.19 = (bf16[96,384]{1,0:T(8,128)(2,1)S(1)}, bf16[96,384]{1,0:T(8,128)(2,1)S(1)}, u32[]{:S(2)}, u32[]{:S(2)}) collective-permute-start(bf16[96,384]{1,0:T(8,128)(2,1)S(1)} %get-tuple-element.74), channel_id=1, source_target_pairs={{0,1},{1,2},{2,3},{3,0},{4,5},{5,6},{6,7},{7,4},{8,9},{9,10},{10,1... | collective-permute-start | bytes 221192 | tf_op jit(solution)/shard_map/ppermute | solution.py:32
  118.6 1.4 collective-permute-done.19
  120.0 1.8 collective-permute-start.20
  121.8 2.2 %collective-permute-start.25 = (bf16[96,384]{1,0:T(8,128)(2,1)S(1)}, bf16[96,384]{1,0:T(8,128)(2,1)S(1)}, u32[]{:S(2)}, u32[]{:S(2)}) collective-permute-start(bf16[96,384]{1,0:T(8,128)(2,1)S(1)} %get-tuple-element.73), channel_id=1, source_target_pairs={{0,12},{1,13},{2,14},{3,15},{4,0},{5,1},{6,2},{7,3},{8,4},{9,5},{1... | collective-permute-start | bytes 221192 | tf_op jit(solution)/shard_map/ppermute | solution.py:32
  124.5 1.5 collective-permute-start.22
  126.0 1.3 collective-permute-start.21
  127.3 2.7 %collective-permute-done.27 = bf16[96,384]{1,0:T(8,128)(2,1)S(1)} collective-permute-done((bf16[96,384]{1,0:T(8,128)(2,1)S(1)}, bf16[96,384]{1,0:T(8,128)(2,1)S(1)}, u32[]{:S(2)}, u32[]{:S(2)}) %collective-permute-start.27) | collective-permute-done | bytes 73760 | tf_op jit(solution)/shard_map/ppermute | solution.py:32
  130.8 2.1 %collective-permute-start.28 = (bf16[4,96,384]{2,1,0:T(8,128)(2,1)S(1)}, bf16[4,96,384]{2,1,0:T(8,128)(2,1)S(1)}, u32[]{:S(2)}, u32[]{:S(2)}) collective-permute-start(bf16[4,96,384]{2,1,0:T(8,128)(2,1)S(1)} %pad_maximum_fusion.3.refs_5_), channel_id=1, source_target_pairs={{0,3},{1,0},{2,1},{3,2},{4,7},{5,4},{6,5},{7,6},{8,11},{9,8},{10,9... | collective-permute-start | bytes 884744 | tf_op jit(solution)/shard_map/ppermute | solution.py:32
  132.8 5.4 %collective-permute-done.22.refs_4_ = bf16[4,96,384]{2,1,0:T(8,128)(2,1)S(1)} collective-permute-done((bf16[4,96,384]{2,1,0:T(8,128)(2,1)S(1)}, bf16[4,96,384]{2,1,0:T(8,128)(2,1)S(1)}, u32[]{:S(2)}, u32[]{:S(2)}) %collective-permute-start.22) | collective-permute-done | bytes 294944 | tf_op jit(solution)/shard_map/ppermute | solution.py:32
  138.6 2.7 %collective-permute-start.24 = (bf16[2,96,384]{2,1,0:T(8,128)(2,1)S(1)}, bf16[2,96,384]{2,1,0:T(8,128)(2,1)S(1)}, u32[]{:S(2)}, u32[]{:S(2)}) collective-permute-start(bf16[2,96,384]{2,1,0:T(8,128)(2,1)S(1)} %slice.62), channel_id=1, source_target_pairs={{0,12},{1,13},{2,14},{3,15},{4,0},{5,1},{6,2},{7,3},{8,4},{9,5},{1... | collective-permute-start | bytes 442376 | tf_op jit(solution)/shard_map/ppermute | solution.py:32
  141.7 1.6 collective-permute-start.30
  143.3 1.3 collective-permute-start.31
  144.6 1.0 collective-permute-done.23.refs_2_
  145.5 3.2 %collective-permute-done.30.refs_7_ = bf16[2,96,384]{2,1,0:T(8,128)(2,1)S(1)} collective-permute-done((bf16[2,96,384]{2,1,0:T(8,128)(2,1)S(1)}, bf16[2,96,384]{2,1,0:T(8,128)(2,1)S(1)}, u32[]{:S(2)}, u32[]{:S(2)}) %collective-permute-start.30) | collective-permute-done | bytes 147488 | tf_op jit(solution)/shard_map/ppermute | solution.py:32
  150.1 4.9 %shard_map.88 = (f32[768,128]{1,0:T(8,128)}, bf16[256,384]{1,0:T(8,128)(2,1)}) custom-call(s32[16]{0:T(128)} %multiply_add_fusion.1.slot_one, s32[16]{0:T(128)} %get-tuple-element.41.slot_two, bf16[4,96,384]{2,1,0:T(8,128)(2,1)} %copy-done.2, bf16[4,96,384]{2,1,0:T(8,128)(2,1)} %copy-done.9, bf16[2,96,384]{2,1,0:T(8,128)(2,1)} %copy-done.20, ...), custom_call_target="tpu_custom_call" | custom-call | tf_op jit(solution)/shard_map/pallas_call | solution.py:279
  155.0 3.8 %collective-permute-start.33 = (bf16[256,384]{1,0:T(8,128)(2,1)}, bf16[256,384]{1,0:T(8,128)(2,1)S(1)}, u32[]{:S(2)}, u32[]{:S(2)}) collective-permute-start(bf16[256,384]{1,0:T(8,128)(2,1)} %get-tuple-element.47.refs_0_), channel_id=1, source_target_pairs={{0,32},{1,33},{2,34},{3,35},{4,36},{5,37},{6,38},{7,39},{8,40},{9,... | collective-permute-start | bytes 589832 | tf_op jit(solution)/shard_map/ppermute | solution.py:32
  158.9 2.4 %collective-permute-start.32 = (bf16[256,384]{1,0:T(8,128)(2,1)}, bf16[256,384]{1,0:T(8,128)(2,1)S(1)}, u32[]{:S(2)}, u32[]{:S(2)}) collective-permute-start(bf16[256,384]{1,0:T(8,128)(2,1)} %get-tuple-element.47.refs_0_), channel_id=1, source_target_pairs={{0,96},{1,97},{2,98},{3,99},{4,100},{5,101},{6,102},{7,103},{8,104... | collective-permute-start | bytes 589832 | tf_op jit(solution)/shard_map/ppermute | solution.py:32
  161.3 4.0 %collective-permute-done.33.refs_4_ = bf16[256,384]{1,0:T(8,128)(2,1)S(1)} collective-permute-done((bf16[256,384]{1,0:T(8,128)(2,1)}, bf16[256,384]{1,0:T(8,128)(2,1)S(1)}, u32[]{:S(2)}, u32[]{:S(2)}) %collective-permute-start.33) | collective-permute-done | bytes 196640 | tf_op jit(solution)/shard_map/ppermute | solution.py:32
  165.4 4.1 %collective-permute-start.34 = (bf16[128,384]{1,0:T(8,128)(2,1)S(1)}, bf16[128,384]{1,0:T(8,128)(2,1)S(1)}, u32[]{:S(2)}, u32[]{:S(2)}) collective-permute-start(bf16[128,384]{1,0:T(8,128)(2,1)S(1)} %slice.66), channel_id=1, source_target_pairs={{0,32},{1,33},{2,34},{3,35},{4,36},{5,37},{6,38},{7,39},{8,40},{9,... | collective-permute-start | bytes 294920 | tf_op jit(solution)/shard_map/ppermute | solution.py:32
  169.5 0.9 collective-permute-start.35
  170.4 2.4 %shard_map.87 = f32[2304,128]{1,0:T(8,128)} custom-call(bf16[768,384]{1,0:T(8,128)(2,1)} %get-tuple-element.39.mine_ref, bf16[768,384]{1,0:T(8,128)(2,1)} %copy-done.12), custom_call_target="tpu_custom_call" | custom-call | tf_op jit(solution)/shard_map/pallas_call | solution.py:279
  172.8 5.1 %collective-permute-done.35.refs_3_ = bf16[128,384]{1,0:T(8,128)(2,1)S(1)} collective-permute-done((bf16[128,384]{1,0:T(8,128)(2,1)S(1)}, bf16[128,384]{1,0:T(8,128)(2,1)S(1)}, u32[]{:S(2)}, u32[]{:S(2)}) %collective-permute-start.35) | collective-permute-done | bytes 98336 | tf_op jit(solution)/shard_map/ppermute | solution.py:32
  177.8 6.5 %collective-permute-start.36 = (bf16[256,384]{1,0:T(8,128)(2,1)}, bf16[256,384]{1,0:T(8,128)(2,1)S(1)}, u32[]{:S(2)}, u32[]{:S(2)}) collective-permute-start(bf16[256,384]{1,0:T(8,128)(2,1)} %get-tuple-element.47.refs_0_), channel_id=1, source_target_pairs={{0,16},{1,17},{2,18},{3,19},{4,20},{5,21},{6,22},{7,23},{8,24},{9,... | collective-permute-start | bytes 589832 | tf_op jit(solution)/shard_map/ppermute | solution.py:32
  187.2 6.2 %shard_map.89 = f32[1024,128]{1,0:T(8,128)} custom-call(s32[16]{0:T(128)} %copy-done.28, s32[8]{0:T(128)} %fusion.5.part_slots, bf16[256,384]{1,0:T(8,128)(2,1)} %get-tuple-element.47.refs_0_, bf16[256,384]{1,0:T(8,128)(2,1)} %copy-done.14, bf16[128,384]{1,0:T(8,128)(2,1)} %copy-done.24, bf16[128,384]{1,0:T(8,128)(2,1)} %copy-done.25, ...), custom_call_target="tpu_custom_call" | custom-call | tf_op jit(solution)/shard_map/pallas_call | solution.py:279
  (152 shorter events, 15.0 us)
Async XLA Ops:
  7.2 95.0 %all-gather.5.cloned.1.call-start = ((), (), s32[]{:S(2)}) async-start(), calls=%async_computation | async-start | bytes 5308416 | tf_op jit(solution)/shard_map/all_gather | solution.py:308
  16.4 170.0 %all-gather.7.cloned.1.call-start = ((), (), s32[]{:S(2)}) async-start(), calls=%async_computation.1 | async-start | bytes 6684672 | tf_op jit(solution)/shard_map/all_gather | solution.py:353
  19.7 10.1 %collective-permute-start.1 = (s32[576,1]{1,0:T(8,128)S(1)}, s32[576,1]{1,0:T(8,128)S(1)}, u32[]{:S(2)}, u32[]{:S(2)}) collective-permute-start(s32[576,1]{1,0:T(8,128)S(1)} %copy.14), channel_id=1, source_target_pairs={{0,128},{1,129},{2,130},{3,131},{4,132},{5,133},{6,134},{7,135},{8... | collective-permute-start | bytes 6920 | tf_op jit(solution)/shard_map/ppermute | solution.py:32
  22.2 17.4 %collective-permute-start = (bf16[768,128]{1,0:T(8,128)(2,1)}, bf16[768,128]{1,0:T(8,128)(2,1)S(1)}, u32[]{:S(2)}, u32[]{:S(2)}) collective-permute-start(bf16[768,128]{1,0:T(8,128)(2,1)} %get-tuple-element.29), channel_id=1, source_target_pairs={{0,0},{1,17},{2,38},{3,55},{4,68},{5,85},{6,98},{7,115},{8,8},{9,2... | collective-permute-start | bytes 589832 | tf_op jit(solution)/shard_map/ppermute | solution.py:32
  27.5 81.0 %copy-start.28 = (s32[16]{0:T(128)}, s32[16]{0:T(128)S(1)}, u32[]{:S(2)}) copy-start(s32[16]{0:T(128)S(1)} %add.201.slots) | copy-start | bytes 196
  29.7 72.4 %copy-start.16 = (s32[576,1]{1,0:T(8,128)}, s32[576,1]{1,0:T(8,128)S(1)}, u32[]{:S(2)}) copy-start(s32[576,1]{1,0:T(8,128)S(1)} %collective-permute-done.1.refs_11_) | copy-start | bytes 6916
  39.6 18.8 %collective-permute-start.3 = (bf16[384,128]{1,0:T(8,128)(2,1)S(1)}, bf16[384,128]{1,0:T(8,128)(2,1)S(1)}, u32[]{:S(2)}, u32[]{:S(2)}) collective-permute-start(bf16[384,128]{1,0:T(8,128)(2,1)S(1)} %get-tuple-element.70), channel_id=1, source_target_pairs={{0,1},{1,2},{2,3},{3,0},{4,5},{5,6},{6,7},{7,4},{8,9},{9,10},{10,1... | collective-permute-start | bytes 294920 | tf_op jit(solution)/shard_map/ppermute | solution.py:32
  39.7 22.7 %collective-permute-start.10 = (bf16[384,128]{1,0:T(8,128)(2,1)S(1)}, bf16[384,128]{1,0:T(8,128)(2,1)S(1)}, u32[]{:S(2)}, u32[]{:S(2)}) collective-permute-start(bf16[384,128]{1,0:T(8,128)(2,1)S(1)} %get-tuple-element.69), channel_id=1, source_target_pairs={{0,4},{1,5},{2,6},{3,7},{4,8},{5,9},{6,10},{7,11},{8,12},{9,13},{1... | collective-permute-start | bytes 294920 | tf_op jit(solution)/shard_map/ppermute | solution.py:32
  43.0 19.4 %collective-permute-start.2 = (bf16[384,128]{1,0:T(8,128)(2,1)S(1)}, bf16[384,128]{1,0:T(8,128)(2,1)S(1)}, u32[]{:S(2)}, u32[]{:S(2)}) collective-permute-start(bf16[384,128]{1,0:T(8,128)(2,1)S(1)} %get-tuple-element.70), channel_id=1, source_target_pairs={{0,3},{1,0},{2,1},{3,2},{4,7},{5,4},{6,5},{7,6},{8,11},{9,8},{10,9... | collective-permute-start | bytes 294920 | tf_op jit(solution)/shard_map/ppermute | solution.py:32
  58.4 5.1 %collective-permute-start.4 = (bf16[384,128]{1,0:T(8,128)(2,1)S(1)}, bf16[384,128]{1,0:T(8,128)(2,1)S(1)}, u32[]{:S(2)}, u32[]{:S(2)}) collective-permute-start(bf16[384,128]{1,0:T(8,128)(2,1)S(1)} %collective-permute-done.3), channel_id=1, source_target_pairs={{0,1},{1,2},{2,3},{3,0},{4,5},{5,6},{6,7},{7,4},{8,9},{9,10},{10,1... | collective-permute-start | bytes 294920 | tf_op jit(solution)/shard_map/ppermute | solution.py:32
  58.4 9.3 %collective-permute-start.9 = (bf16[384,128]{1,0:T(8,128)(2,1)S(1)}, bf16[384,128]{1,0:T(8,128)(2,1)S(1)}, u32[]{:S(2)}, u32[]{:S(2)}) collective-permute-start(bf16[384,128]{1,0:T(8,128)(2,1)S(1)} %get-tuple-element.69), channel_id=1, source_target_pairs={{0,12},{1,13},{2,14},{3,15},{4,0},{5,1},{6,2},{7,3},{8,4},{9,5},{1... | collective-permute-start | bytes 294920 | tf_op jit(solution)/shard_map/ppermute | solution.py:32
  62.4 5.3 %collective-permute-start.11 = (bf16[384,128]{1,0:T(8,128)(2,1)S(1)}, bf16[384,128]{1,0:T(8,128)(2,1)S(1)}, u32[]{:S(2)}, u32[]{:S(2)}) collective-permute-start(bf16[384,128]{1,0:T(8,128)(2,1)S(1)} %collective-permute-done.10), channel_id=1, source_target_pairs={{0,4},{1,5},{2,6},{3,7},{4,8},{5,9},{6,10},{7,11},{8,12},{9,13},{1... | collective-permute-start | bytes 294920 | tf_op jit(solution)/shard_map/ppermute | solution.py:32
  63.6 38.6 %copy-start = (bf16[4,384,128]{2,1,0:T(8,128)(2,1)}, bf16[4,384,128]{2,1,0:T(8,128)(2,1)S(1)}, u32[]{:S(2)}) copy-start(bf16[4,384,128]{2,1,0:T(8,128)(2,1)S(1)} %pad_maximum_fusion.refs_0_) | copy-start | bytes 1179652
  63.6 13.2 %collective-permute-start.6 = (bf16[4,384,128]{2,1,0:T(8,128)(2,1)S(1)}, bf16[4,384,128]{2,1,0:T(8,128)(2,1)S(1)}, u32[]{:S(2)}, u32[]{:S(2)}) collective-permute-start(bf16[4,384,128]{2,1,0:T(8,128)(2,1)S(1)} %pad_maximum_fusion.refs_0_), channel_id=1, source_target_pairs={{0,4},{1,5},{2,6},{3,7},{4,8},{5,9},{6,10},{7,11},{8,12},{9,13},{1... | collective-permute-start | bytes 1179656 | tf_op jit(solution)/shard_map/ppermute | solution.py:32
  65.9 14.7 %collective-permute-start.5 = (bf16[4,384,128]{2,1,0:T(8,128)(2,1)S(1)}, bf16[4,384,128]{2,1,0:T(8,128)(2,1)S(1)}, u32[]{:S(2)}, u32[]{:S(2)}) collective-permute-start(bf16[4,384,128]{2,1,0:T(8,128)(2,1)S(1)} %pad_maximum_fusion.refs_0_), channel_id=1, source_target_pairs={{0,12},{1,13},{2,14},{3,15},{4,0},{5,1},{6,2},{7,3},{8,4},{9,5},{1... | collective-permute-start | bytes 1179656 | tf_op jit(solution)/shard_map/ppermute | solution.py:32
  67.8 34.4 %copy-start.1 = (bf16[4,384,128]{2,1,0:T(8,128)(2,1)}, bf16[4,384,128]{2,1,0:T(8,128)(2,1)S(1)}, u32[]{:S(2)}) copy-start(bf16[4,384,128]{2,1,0:T(8,128)(2,1)S(1)} %pad_maximum_fusion.1.refs_5_) | copy-start | bytes 1179652
  67.8 13.0 %collective-permute-start.13 = (bf16[4,384,128]{2,1,0:T(8,128)(2,1)S(1)}, bf16[4,384,128]{2,1,0:T(8,128)(2,1)S(1)}, u32[]{:S(2)}, u32[]{:S(2)}) collective-permute-start(bf16[4,384,128]{2,1,0:T(8,128)(2,1)S(1)} %pad_maximum_fusion.1.refs_5_), channel_id=1, source_target_pairs={{0,1},{1,2},{2,3},{3,0},{4,5},{5,6},{6,7},{7,4},{8,9},{9,10},{10,1... | collective-permute-start | bytes 1179656 | tf_op jit(solution)/shard_map/ppermute | solution.py:32
  67.9 13.7 %collective-permute-start.12 = (bf16[4,384,128]{2,1,0:T(8,128)(2,1)S(1)}, bf16[4,384,128]{2,1,0:T(8,128)(2,1)S(1)}, u32[]{:S(2)}, u32[]{:S(2)}) collective-permute-start(bf16[4,384,128]{2,1,0:T(8,128)(2,1)S(1)} %pad_maximum_fusion.1.refs_5_), channel_id=1, source_target_pairs={{0,3},{1,0},{2,1},{3,2},{4,7},{5,4},{6,5},{7,6},{8,11},{9,8},{10,9... | collective-permute-start | bytes 1179656 | tf_op jit(solution)/shard_map/ppermute | solution.py:32
  70.5 38.0 %collective-permute-start.41 = (bf16[1536,128]{1,0:T(8,128)(2,1)}, bf16[1536,128]{1,0:T(8,128)(2,1)S(1)}, u32[]{:S(2)}, u32[]{:S(2)}) collective-permute-start(bf16[1536,128]{1,0:T(8,128)(2,1)} %get-tuple-element.53), channel_id=1, source_target_pairs={{0,0},{1,17},{2,38},{3,55},{4,68},{5,85},{6,98},{7,115},{8,8},{9,2... | collective-permute-start | bytes 1179656 | tf_op jit(solution)/shard_map/ppermute | solution.py:32
  76.9 9.0 %collective-permute-start.7 = (bf16[2,384,128]{2,1,0:T(8,128)(2,1)S(1)}, bf16[2,384,128]{2,1,0:T(8,128)(2,1)}, u32[]{:S(2)}, u32[]{:S(2)}) collective-permute-start(bf16[2,384,128]{2,1,0:T(8,128)(2,1)S(1)} %slice.56), channel_id=1, source_target_pairs={{0,4},{1,5},{2,6},{3,7},{4,8},{5,9},{6,10},{7,11},{8,12},{9,13},{1... | collective-permute-start | bytes 589832 | tf_op jit(solution)/shard_map/ppermute | solution.py:32
  80.6 5.2 %collective-permute-start.8 = (bf16[2,384,128]{2,1,0:T(8,128)(2,1)S(1)}, bf16[2,384,128]{2,1,0:T(8,128)(2,1)}, u32[]{:S(2)}, u32[]{:S(2)}) collective-permute-start(bf16[2,384,128]{2,1,0:T(8,128)(2,1)S(1)} %slice.57), channel_id=1, source_target_pairs={{0,12},{1,13},{2,14},{3,15},{4,0},{5,1},{6,2},{7,3},{8,4},{9,5},{1... | collective-permute-start | bytes 589832 | tf_op jit(solution)/shard_map/ppermute | solution.py:32
  81.5 12.3 %collective-permute-start.14 = (bf16[2,384,128]{2,1,0:T(8,128)(2,1)}, bf16[2,384,128]{2,1,0:T(8,128)(2,1)}, u32[]{:S(2)}, u32[]{:S(2)}) collective-permute-start(bf16[2,384,128]{2,1,0:T(8,128)(2,1)} %slice.58), channel_id=1, source_target_pairs={{0,1},{1,2},{2,3},{3,0},{4,5},{5,6},{6,7},{7,4},{8,9},{9,10},{10,1... | collective-permute-start | bytes 589832 | tf_op jit(solution)/shard_map/ppermute | solution.py:32
  82.3 11.5 %collective-permute-start.15 = (bf16[2,384,128]{2,1,0:T(8,128)(2,1)}, bf16[2,384,128]{2,1,0:T(8,128)(2,1)}, u32[]{:S(2)}, u32[]{:S(2)}) collective-permute-start(bf16[2,384,128]{2,1,0:T(8,128)(2,1)} %slice.59), channel_id=1, source_target_pairs={{0,3},{1,0},{2,1},{3,2},{4,7},{5,4},{6,5},{7,6},{8,11},{9,8},{10,9... | collective-permute-start | bytes 589832 | tf_op jit(solution)/shard_map/ppermute | solution.py:32
  109.3 4.3 %collective-permute-start.16 = (bf16[192,384]{1,0:T(8,128)(2,1)}, bf16[192,384]{1,0:T(8,128)(2,1)S(1)}, u32[]{:S(2)}, u32[]{:S(2)}) collective-permute-start(bf16[192,384]{1,0:T(8,128)(2,1)} %get-tuple-element.38), channel_id=1, source_target_pairs={{0,128},{1,129},{2,130},{3,131},{4,132},{5,133},{6,134},{7,135},{8... | collective-permute-start | bytes 442376 | tf_op jit(solution)/shard_map/ppermute | solution.py:32
  114.6 5.4 %collective-permute-start.19 = (bf16[96,384]{1,0:T(8,128)(2,1)S(1)}, bf16[96,384]{1,0:T(8,128)(2,1)S(1)}, u32[]{:S(2)}, u32[]{:S(2)}) collective-permute-start(bf16[96,384]{1,0:T(8,128)(2,1)S(1)} %get-tuple-element.74), channel_id=1, source_target_pairs={{0,1},{1,2},{2,3},{3,0},{4,5},{5,6},{6,7},{7,4},{8,9},{9,10},{10,1... | collective-permute-start | bytes 221192 | tf_op jit(solution)/shard_map/ppermute | solution.py:32
  118.6 5.7 %collective-permute-start.26 = (bf16[96,384]{1,0:T(8,128)(2,1)S(1)}, bf16[96,384]{1,0:T(8,128)(2,1)S(1)}, u32[]{:S(2)}, u32[]{:S(2)}) collective-permute-start(bf16[96,384]{1,0:T(8,128)(2,1)S(1)} %get-tuple-element.73), channel_id=1, source_target_pairs={{0,4},{1,5},{2,6},{3,7},{4,8},{5,9},{6,10},{7,11},{8,12},{9,13},{1... | collective-permute-start | bytes 221192 | tf_op jit(solution)/shard_map/ppermute | solution.py:32
  118.6 5.7 %collective-permute-start.18 = (bf16[96,384]{1,0:T(8,128)(2,1)S(1)}, bf16[96,384]{1,0:T(8,128)(2,1)S(1)}, u32[]{:S(2)}, u32[]{:S(2)}) collective-permute-start(bf16[96,384]{1,0:T(8,128)(2,1)S(1)} %get-tuple-element.74), channel_id=1, source_target_pairs={{0,3},{1,0},{2,1},{3,2},{4,7},{5,4},{6,5},{7,6},{8,11},{9,8},{10,9... | collective-permute-start | bytes 221192 | tf_op jit(solution)/shard_map/ppermute | solution.py:32
  120.0 4.4 %collective-permute-start.20 = (bf16[96,384]{1,0:T(8,128)(2,1)S(1)}, bf16[96,384]{1,0:T(8,128)(2,1)S(1)}, u32[]{:S(2)}, u32[]{:S(2)}) collective-permute-start(bf16[96,384]{1,0:T(8,128)(2,1)S(1)} %collective-permute-done.19), channel_id=1, source_target_pairs={{0,1},{1,2},{2,3},{3,0},{4,5},{5,6},{6,7},{7,4},{8,9},{9,10},{10,1... | collective-permute-start | bytes 221192 | tf_op jit(solution)/shard_map/ppermute | solution.py:32
  121.8 5.5 %collective-permute-start.25 = (bf16[96,384]{1,0:T(8,128)(2,1)S(1)}, bf16[96,384]{1,0:T(8,128)(2,1)S(1)}, u32[]{:S(2)}, u32[]{:S(2)}) collective-permute-start(bf16[96,384]{1,0:T(8,128)(2,1)S(1)} %get-tuple-element.73), channel_id=1, source_target_pairs={{0,12},{1,13},{2,14},{3,15},{4,0},{5,1},{6,2},{7,3},{8,4},{9,5},{1... | collective-permute-start | bytes 221192 | tf_op jit(solution)/shard_map/ppermute | solution.py:32
  124.0 31.0 %collective-permute-start.17 = (bf16[768,384]{1,0:T(8,128)(2,1)}, bf16[768,384]{1,0:T(8,128)(2,1)S(1)}, u32[]{:S(2)}, u32[]{:S(2)}) collective-permute-start(bf16[768,384]{1,0:T(8,128)(2,1)} %get-tuple-element.39.mine_ref), channel_id=1, source_target_pairs={{0,128},{1,129},{2,130},{3,131},{4,132},{5,133},{6,134},{7,135},{8... | collective-permute-start | bytes 1769480 | tf_op jit(solution)/shard_map/ppermute | solution.py:32
  124.4 5.7 %collective-permute-start.27 = (bf16[96,384]{1,0:T(8,128)(2,1)S(1)}, bf16[96,384]{1,0:T(8,128)(2,1)S(1)}, u32[]{:S(2)}, u32[]{:S(2)}) collective-permute-start(bf16[96,384]{1,0:T(8,128)(2,1)S(1)} %collective-permute-done.26), channel_id=1, source_target_pairs={{0,4},{1,5},{2,6},{3,7},{4,8},{5,9},{6,10},{7,11},{8,12},{9,13},{1... | collective-permute-start | bytes 221192 | tf_op jit(solution)/shard_map/ppermute | solution.py:32
  124.5 13.7 %collective-permute-start.22 = (bf16[4,96,384]{2,1,0:T(8,128)(2,1)S(1)}, bf16[4,96,384]{2,1,0:T(8,128)(2,1)S(1)}, u32[]{:S(2)}, u32[]{:S(2)}) collective-permute-start(bf16[4,96,384]{2,1,0:T(8,128)(2,1)S(1)} %pad_maximum_fusion.2.refs_0_), channel_id=1, source_target_pairs={{0,4},{1,5},{2,6},{3,7},{4,8},{5,9},{6,10},{7,11},{8,12},{9,13},{1... | collective-permute-start | bytes 884744 | tf_op jit(solution)/shard_map/ppermute | solution.py:32
  126.0 12.6 %collective-permute-start.21 = (bf16[4,96,384]{2,1,0:T(8,128)(2,1)S(1)}, bf16[4,96,384]{2,1,0:T(8,128)(2,1)S(1)}, u32[]{:S(2)}, u32[]{:S(2)}) collective-permute-start(bf16[4,96,384]{2,1,0:T(8,128)(2,1)S(1)} %pad_maximum_fusion.2.refs_0_), channel_id=1, source_target_pairs={{0,12},{1,13},{2,14},{3,15},{4,0},{5,1},{6,2},{7,3},{8,4},{9,5},{1... | collective-permute-start | bytes 884744 | tf_op jit(solution)/shard_map/ppermute | solution.py:32
  130.1 11.6 %collective-permute-start.29 = (bf16[4,96,384]{2,1,0:T(8,128)(2,1)S(1)}, bf16[4,96,384]{2,1,0:T(8,128)(2,1)S(1)}, u32[]{:S(2)}, u32[]{:S(2)}) collective-permute-start(bf16[4,96,384]{2,1,0:T(8,128)(2,1)S(1)} %pad_maximum_fusion.3.refs_5_), channel_id=1, source_target_pairs={{0,1},{1,2},{2,3},{3,0},{4,5},{5,6},{6,7},{7,4},{8,9},{9,10},{10,1... | collective-permute-start | bytes 884744 | tf_op jit(solution)/shard_map/ppermute | solution.py:32
  130.8 12.5 %collective-permute-start.28 = (bf16[4,96,384]{2,1,0:T(8,128)(2,1)S(1)}, bf16[4,96,384]{2,1,0:T(8,128)(2,1)S(1)}, u32[]{:S(2)}, u32[]{:S(2)}) collective-permute-start(bf16[4,96,384]{2,1,0:T(8,128)(2,1)S(1)} %pad_maximum_fusion.3.refs_5_), channel_id=1, source_target_pairs={{0,3},{1,0},{2,1},{3,2},{4,7},{5,4},{6,5},{7,6},{8,11},{9,8},{10,9... | collective-permute-start | bytes 884744 | tf_op jit(solution)/shard_map/ppermute | solution.py:32
  138.2 7.3 %collective-permute-start.23 = (bf16[2,96,384]{2,1,0:T(8,128)(2,1)S(1)}, bf16[2,96,384]{2,1,0:T(8,128)(2,1)S(1)}, u32[]{:S(2)}, u32[]{:S(2)}) collective-permute-start(bf16[2,96,384]{2,1,0:T(8,128)(2,1)S(1)} %slice.61), channel_id=1, source_target_pairs={{0,4},{1,5},{2,6},{3,7},{4,8},{5,9},{6,10},{7,11},{8,12},{9,13},{1... | collective-permute-start | bytes 442376 | tf_op jit(solution)/shard_map/ppermute | solution.py:32
  138.6 6.9 %collective-permute-start.24 = (bf16[2,96,384]{2,1,0:T(8,128)(2,1)S(1)}, bf16[2,96,384]{2,1,0:T(8,128)(2,1)S(1)}, u32[]{:S(2)}, u32[]{:S(2)}) collective-permute-start(bf16[2,96,384]{2,1,0:T(8,128)(2,1)S(1)} %slice.62), channel_id=1, source_target_pairs={{0,12},{1,13},{2,14},{3,15},{4,0},{5,1},{6,2},{7,3},{8,4},{9,5},{1... | collective-permute-start | bytes 442376 | tf_op jit(solution)/shard_map/ppermute | solution.py:32
  141.7 7.1 %collective-permute-start.30 = (bf16[2,96,384]{2,1,0:T(8,128)(2,1)S(1)}, bf16[2,96,384]{2,1,0:T(8,128)(2,1)S(1)}, u32[]{:S(2)}, u32[]{:S(2)}) collective-permute-start(bf16[2,96,384]{2,1,0:T(8,128)(2,1)S(1)} %slice.64), channel_id=1, source_target_pairs={{0,1},{1,2},{2,3},{3,0},{4,5},{5,6},{6,7},{7,4},{8,9},{9,10},{10,1... | collective-permute-start | bytes 442376 | tf_op jit(solution)/shard_map/ppermute | solution.py:32
  143.3 5.7 %collective-permute-start.31 = (bf16[2,96,384]{2,1,0:T(8,128)(2,1)S(1)}, bf16[2,96,384]{2,1,0:T(8,128)(2,1)S(1)}, u32[]{:S(2)}, u32[]{:S(2)}) collective-permute-start(bf16[2,96,384]{2,1,0:T(8,128)(2,1)S(1)} %slice.65), channel_id=1, source_target_pairs={{0,3},{1,0},{2,1},{3,2},{4,7},{5,4},{6,5},{7,6},{8,11},{9,8},{10,9... | collective-permute-start | bytes 442376 | tf_op jit(solution)/shard_map/ppermute | solution.py:32
  155.0 10.3 %collective-permute-start.33 = (bf16[256,384]{1,0:T(8,128)(2,1)}, bf16[256,384]{1,0:T(8,128)(2,1)S(1)}, u32[]{:S(2)}, u32[]{:S(2)}) collective-permute-start(bf16[256,384]{1,0:T(8,128)(2,1)} %get-tuple-element.47.refs_0_), channel_id=1, source_target_pairs={{0,32},{1,33},{2,34},{3,35},{4,36},{5,37},{6,38},{7,39},{8,40},{9,... | collective-permute-start | bytes 589832 | tf_op jit(solution)/shard_map/ppermute | solution.py:32
  158.9 10.6 %collective-permute-start.32 = (bf16[256,384]{1,0:T(8,128)(2,1)}, bf16[256,384]{1,0:T(8,128)(2,1)S(1)}, u32[]{:S(2)}, u32[]{:S(2)}) collective-permute-start(bf16[256,384]{1,0:T(8,128)(2,1)} %get-tuple-element.47.refs_0_), channel_id=1, source_target_pairs={{0,96},{1,97},{2,98},{3,99},{4,100},{5,101},{6,102},{7,103},{8,104... | collective-permute-start | bytes 589832 | tf_op jit(solution)/shard_map/ppermute | solution.py:32
  165.4 7.4 %collective-permute-start.34 = (bf16[128,384]{1,0:T(8,128)(2,1)S(1)}, bf16[128,384]{1,0:T(8,128)(2,1)S(1)}, u32[]{:S(2)}, u32[]{:S(2)}) collective-permute-start(bf16[128,384]{1,0:T(8,128)(2,1)S(1)} %slice.66), channel_id=1, source_target_pairs={{0,32},{1,33},{2,34},{3,35},{4,36},{5,37},{6,38},{7,39},{8,40},{9,... | collective-permute-start | bytes 294920 | tf_op jit(solution)/shard_map/ppermute | solution.py:32
  169.5 8.3 %collective-permute-start.35 = (bf16[128,384]{1,0:T(8,128)(2,1)S(1)}, bf16[128,384]{1,0:T(8,128)(2,1)S(1)}, u32[]{:S(2)}, u32[]{:S(2)}) collective-permute-start(bf16[128,384]{1,0:T(8,128)(2,1)S(1)} %slice.67), channel_id=1, source_target_pairs={{0,96},{1,97},{2,98},{3,99},{4,100},{5,101},{6,102},{7,103},{8,104... | collective-permute-start | bytes 294920 | tf_op jit(solution)/shard_map/ppermute | solution.py:32
  177.8 8.5 %collective-permute-start.36 = (bf16[256,384]{1,0:T(8,128)(2,1)}, bf16[256,384]{1,0:T(8,128)(2,1)S(1)}, u32[]{:S(2)}, u32[]{:S(2)}) collective-permute-start(bf16[256,384]{1,0:T(8,128)(2,1)} %get-tuple-element.47.refs_0_), channel_id=1, source_target_pairs={{0,16},{1,17},{2,18},{3,19},{4,20},{5,21},{6,22},{7,23},{8,24},{9,... | collective-permute-start | bytes 589832 | tf_op jit(solution)/shard_map/ppermute | solution.py:32
  184.3 2.0 %collective-permute-start.37 = (bf16[256,384]{1,0:T(8,128)(2,1)S(1)}, bf16[256,384]{1,0:T(8,128)(2,1)S(1)}, u32[]{:S(2)}, u32[]{:S(2)}) collective-permute-start(bf16[256,384]{1,0:T(8,128)(2,1)S(1)} %collective-permute-done.32.refs_1_), channel_id=1, source_target_pairs={{0,16},{1,17},{2,18},{3,19},{4,20},{5,21},{6,22},{7,23},{8,24},{9,... | collective-permute-start | bytes 589832 | tf_op jit(solution)/shard_map/ppermute | solution.py:32
  184.4 1.9 collective-permute-start.40
  184.8 1.4 collective-permute-start.38
  184.9 1.4 collective-permute-start.39
  (25 other events, 254.8 us)
Sparse Core Ops, SparseCore 0:
  16.5 85.5 all-gather.4
  109.4 73.0 all-gather.6
